TPU v7x, 256 devices: a whole 4x4x8 slice. The times are simulated.
256 devices in a mesh: prow: 8 (over z_hi, core), pcol: 32 (over x, y, z_lo).
Axes of the slice: x: 4, y: 4, z: 8 (z_hi: 4, z_lo: 2; z = z_hi * 2 + z_lo), core: 2. Of those that a mesh axis runs over, the one named last changes fastest.
Arguments:
- inverse_anc: float32 [8192, 8192], P('prow', 'pcol'), as said below
- lower_two: float32 [8192, 2048], P('prow', 'pcol'), may hold values from -1.5 to 1.5
- pattern_two: int32 [32, 8], replicated, may hold values 0 or 1
- widths_two: int32 [8], replicated, may hold values from 64 to 256
- dinv_two: float32 [8, 256, 256], P('prow'), may hold values from -6 to 6
- lower_one: float32 [8192, 2048], P('prow', 'pcol'), may hold values from -1.5 to 1.5
- pattern_one: int32 [32, 8], replicated, may hold values 0 or 1
- widths_one: int32 [8], replicated, may hold values from 64 to 256
- parent_one: int32 [8], replicated, may hold values from 0 to 7
- lower_par: float32 [8, 256, 256], P('prow'), may hold values from -0.3 to 0.3
- dinv_one: float32 [8, 256, 256], P('prow'), may hold values from -6 to 6
Outputs:
- upper_two: float32 [2048, 8192], P('prow', 'pcol')
- diag_two: float32 [8, 256, 256], P('prow')
- upper_one: float32 [2048, 8192], P('prow', 'pcol')
- parent_block: float32 [8, 256, 256], P('prow')
- diag_one: float32 [8, 256, 256], P('prow')
Inputs may be any that keep to these rules, and one draw needn't show every extreme that they name: inverse_anc is symmetric.
All inputs are finite; a program needn't handle non-finite values.
Results may differ from a plain program's by a relative error of at most 0.00011.
Values sent between devices are 32-bit elements; how exact they have to be, the bound alone decides.
A program may use at most 128 MiB of HBM per device.

v0:
```python
import jax
import jax.numpy as jnp
from jax import lax
from jax.sharding import PartitionSpec as P

B = 256


HIGH = lax.Precision.HIGHEST


def broadcast(value, axis, source):
    kept = jnp.where(lax.axis_index(axis) == source, value, 0).astype(value.dtype)
    return lax.psum(kept, axis)


def shard_mask(pattern, widths, row_index, col_index, rows_dev, cols_dev):
    count = pattern.shape[1]
    nblocks = rows_dev // B
    pat_rows = lax.dynamic_slice_in_dim(pattern, row_index * nblocks, nblocks, 0)
    pat_full = jnp.repeat(pat_rows.astype(jnp.float32), B, axis=0)
    columns = col_index * cols_dev + jnp.arange(cols_dev, dtype=jnp.int32)
    owner = columns // B
    onehot = (owner[None, :] == jnp.arange(count, dtype=jnp.int32)[:, None]).astype(jnp.float32)
    block_mask = jnp.dot(pat_full, onehot, precision=HIGH, preferred_element_type=jnp.float32)
    width_col = jnp.sum(onehot * widths.astype(jnp.float32)[:, None], axis=0)
    keep = ((columns % B).astype(jnp.float32) < width_col).astype(jnp.float32)
    return block_mask * keep[None, :]


def left_product(piece, inverse_anc):
    return lax.dot_general(
        piece,
        inverse_anc,
        (((0,), (0,)), ((), ())),
        precision=HIGH,
        preferred_element_type=jnp.float32,
    )


def per_device(
    inverse_anc,
    lower_two,
    pattern_two,
    widths_two,
    dinv_two,
    lower_one,
    pattern_one,
    widths_one,
    parent_one,
    lower_par,
    dinv_one,
):
    rows_count = lax.axis_size("prow")
    cols_count = lax.axis_size("pcol")
    row_index = lax.axis_index("prow")
    col_index = lax.axis_index("pcol")
    rows_dev, cols_dev = inverse_anc.shape
    width_two = lower_two.shape[1]
    total_cols = width_two * cols_count
    share = total_cols // rows_count
    local_sup = dinv_two.shape[0]
    lmat_two = lower_two * shard_mask(
        pattern_two, widths_two, row_index, col_index, rows_dev, width_two
    )
    lmat_one = lower_one * shard_mask(
        pattern_one, widths_one, row_index, col_index, rows_dev, width_two
    )
    owner_row = col_index * rows_count // cols_count
    offset = col_index * cols_dev - owner_row * rows_dev
    rows_two = lax.all_gather(lmat_two, "pcol", axis=1, tiled=True)
    upper_two = -lax.psum_scatter(
        left_product(rows_two, inverse_anc), "prow", scatter_dimension=0, tiled=True
    )
    cols_two = broadcast(lax.dynamic_slice_in_dim(rows_two, offset, cols_dev, 0), "prow", owner_row)
    rows_one = lax.all_gather(lmat_one, "pcol", axis=1, tiled=True)
    main_one = -lax.psum_scatter(
        left_product(rows_one, inverse_anc), "prow", scatter_dimension=0, tiled=True
    )
    cols_one = broadcast(lax.dynamic_slice_in_dim(rows_one, offset, cols_dev, 0), "prow", owner_row)
    mine_two = lax.dynamic_slice_in_dim(cols_two, row_index * share, share, 1).reshape(
        cols_dev, local_sup, B
    )
    mine_one = lax.dynamic_slice_in_dim(cols_one, row_index * share, share, 1).reshape(
        cols_dev, local_sup, B
    )
    upper_two_blocks = upper_two.reshape(local_sup, B, cols_dev)
    part_two = jnp.einsum("inb,nci->nbc", mine_two, upper_two_blocks, precision=HIGH)
    diag_two = dinv_two - lax.psum(part_two, "pcol")
    every_upper, every_diag = (
        lax.all_gather(upper_two, "prow", axis=0, tiled=True),
        lax.all_gather(diag_two, "prow", axis=0, tiled=True),
    )
    all_sup = every_diag.shape[0]
    parent_local = lax.dynamic_slice_in_dim(parent_one, row_index * local_sup, local_sup, 0)
    select = (parent_local[:, None] == jnp.arange(all_sup, dtype=jnp.int32)[None, :]).astype(
        jnp.float32
    )
    parent_rows = jnp.einsum(
        "nm,mbi->nbi", select, every_upper.reshape(all_sup, B, cols_dev), precision=HIGH
    )
    parent_diag = jnp.einsum("nm,mbc->nbc", select, every_diag, precision=HIGH)
    parent_width = jnp.sum(select * widths_two.astype(jnp.float32)[None, :], axis=1)
    own_width = lax.dynamic_slice_in_dim(widths_one, row_index * local_sup, local_sup, 0).astype(
        jnp.float32
    )
    inner = jnp.arange(B, dtype=jnp.int32).astype(jnp.float32)
    row_keep = (inner[None, :] < parent_width[:, None]).astype(jnp.float32)
    col_keep = (inner[None, :] < own_width[:, None]).astype(jnp.float32)
    lpar = lower_par * row_keep[:, :, None] * col_keep[:, None, :]
    upper_one_blocks = main_one.reshape(local_sup, B, cols_dev) - jnp.einsum(
        "nbc,nbi->nci", lpar, parent_rows, precision=HIGH
    )
    first_part = jnp.einsum("nbi,inc->nbc", parent_rows, mine_one, precision=HIGH)
    second_part = jnp.einsum("inb,nci->nbc", mine_one, upper_one_blocks, precision=HIGH)
    first_sum, second_sum = lax.psum((first_part, second_part), "pcol")
    parent_block = -first_sum - jnp.einsum("nbc,ncd->nbd", parent_diag, lpar, precision=HIGH)
    diag_one = (
        dinv_one - second_sum - jnp.einsum("nbc,nbd->ncd", lpar, parent_block, precision=HIGH)
    )
    return (upper_two, diag_two, upper_one_blocks.reshape(share, cols_dev), parent_block, diag_one)


def solution(mesh):
    in_specs = (
        P("prow", "pcol"),
        P("prow", "pcol"),
        P(),
        P(),
        P("prow", None, None),
        P("prow", "pcol"),
        P(),
        P(),
        P(),
        P("prow", None, None),
        P("prow", None, None),
    )
    out_specs = (
        P("prow", "pcol"),
        P("prow", None, None),
        P("prow", "pcol"),
        P("prow", None, None),
        P("prow", None, None),
    )
    return jax.shard_map(
        per_device, mesh=mesh, in_specs=in_specs, out_specs=out_specs, check_vma=False
    )
```

profile of v0, /device:TPU:4, one launch (start us, length us, event | category | flops | bytes accessed | tf_op | source)
XLA Modules:
  0.0 1014.8 jit_solution(1391687690577915184)
XLA Ops:
  7.2 0.9 dynamic-slice_convert_fusion
  8.2 0.7 convert_element_type.85
  8.9 0.7 convert_element_type.82
  9.7 2.1 fusion.5
  12.0 1.2 fusion.4
  13.3 192.2 %all-gather.5.cloned.1.call-done = f32[1024,2048]{0,1:T(8,128)} async-done(((f32[1024,64]{0,1:T(8,128)}), f32[1024,2048]{0,1:T(8,128)}) %all-gather.5.cloned.1.call-update) | async-done | bytes 8388624 | tf_op jit(solution)/shard_map/all_gather | solution.py:71
  205.5 10.0 fusion.42
  215.6 3.1 dynamic-slice_select_fusion.1
  218.6 179.2 %all-gather.7.cloned.1.call-done = f32[1024,2048]{0,1:T(8,128)} async-done(((f32[1024,64]{0,1:T(8,128)}), f32[1024,2048]{0,1:T(8,128)}) %all-gather.7.cloned.1.call-update) | async-done | bytes 8388624 | tf_op jit(solution)/shard_map/all_gather | solution.py:76
  397.8 3.1 dynamic-slice_select_fusion
  400.9 42.2 %reduce-scatter.3.cloned.1.call-done = f32[256,256]{1,0:T(8,128)} async-done(((f32[2048,256]{1,0:T(8,128)}), f32[256,256]{1,0:T(8,128)}) %reduce-scatter.3.cloned.1.call-update) | async-done | bytes 262160 | tf_op jit(solution)/shard_map/reduce_scatter | solution.py:72
  443.1 1.7 neg.9
  444.9 10.0 fusion.43
  455.2 0.4 copy-done.10
  455.5 0.6 dynamic_slice.29
  456.1 0.6 dynamic_slice.28
  457.4 1.2 fusion.37
  458.6 0.6 compare_convert_fusion
  459.3 105.3 %all-reduce.7.cloned.1.call-done = (f32[256,2048]{0,1:T(8,128)}, f32[256,2048]{0,1:T(8,128)}) async-done(((f32[256,2048]{0,1:T(8,128)}, f32[256,2048]{0,1:T(8,128)}), (f32[256,2048]{0,1:T(8,128)}, f32[256,2048]{0,1:T(8,128)})) %all-reduce.7.cloned.1.call-update) | async-done | bytes 4194320 | tf_op jit(solution)/shard_map/psum | solution.py:14
  564.6 2.1 convolution_bitcast_fusion.4
  566.6 36.6 %all-gather.9.cloned.1.call-done = f32[2048,256]{1,0:T(8,128)} async-done(((f32[256,256]{1,0:T(8,128)}), f32[2048,256]{1,0:T(8,128)}) %all-gather.9.cloned.1.call-update) | async-done | bytes 2097168 | tf_op jit(solution)/shard_map/all_gather | solution.py:91
  603.3 4.4 fusion.2
  607.7 2.1 convolution_bitcast_fusion.3
  609.8 37.0 %reduce-scatter.5.cloned.1.call-done = f32[256,256]{1,0:T(8,128)} async-done(((f32[2048,256]{1,0:T(8,128)}), f32[256,256]{1,0:T(8,128)}) %reduce-scatter.5.cloned.1.call-update) | async-done | bytes 262160 | tf_op jit(solution)/shard_map/reduce_scatter | solution.py:77
  646.8 1.6 convolution_subtract_fusion
  648.4 2.2 convolution_bitcast_fusion.1
  650.7 294.2 %all-reduce.5.cloned.1.call-done = (f32[1,256,256]{2,1,0:T(8,128)}, f32[1,256,256]{2,1,0:T(8,128)}, f32[1,256,256]{2,1,0:T(8,128)}) async-done(((f32[1,256,256]{2,1,0:T(8,128)}, f32[1,256,256]{2,1,0:T(8,128)}, f32[1,256,256]{2,1,0:T(8,128)}), (f32[1,256,256]{2,1,0:T(8,128)}, f32[1,256,256]{2,1,0:T(8,128)}, f32[1,256,256]{2,1,0:T(8,128)})) %all-reduce.5.cloned.1.call-update) | async-done | bytes 786448 | tf_op jit(solution)/shard_map/psum | solution.py:89
  944.9 1.8 sub.34
  946.7 55.0 %all-gather.11.cloned.1.call-done = f32[8,256,256]{2,1,0:T(8,128)} async-done(((f32[1,256,256]{2,1,0:T(8,128)}), f32[8,256,256]{2,1,0:T(8,128)}) %all-gather.11.cloned.1.call-update) | async-done | bytes 2097168 | tf_op jit(solution)/shard_map/all_gather | solution.py:92
  1001.6 4.4 fusion
  1006.1 0.5 fusion.6
  1006.6 1.4 fusion.7
  (49 shorter events, 1.1 us)
Async XLA Ops:
  7.2 198.3 %copy-start = (f32[1024,256]{1,0:T(8,128)S(1)}, f32[1024,256]{1,0:T(8,128)}, u32[]{:S(2)}) copy-start(f32[1024,256]{1,0:T(8,128)} %param.11) | copy-start | bytes 3145732
  7.2 4.8 copy-start.5
  7.2 198.3 %all-gather.5.cloned.1.call-start = ((), (), s32[]{:S(2)}) async-start(), calls=%async_computation.2 | async-start | bytes 8650752 | tf_op jit(solution)/shard_map/all_gather | solution.py:71
  11.8 386.0 %all-gather.7.cloned.1.call-start = ((), (), s32[]{:S(2)}) async-start(), calls=%async_computation.4 | async-start | bytes 8650752 | tf_op jit(solution)/shard_map/all_gather | solution.py:76
  13.2 429.9 %reduce-scatter.3.cloned.1.call-start = ((), (), s32[]{:S(2)}) async-start(), calls=%async_computation.3 | async-start | bytes 2359296 | tf_op jit(solution)/shard_map/reduce_scatter | solution.py:72
  215.5 349.1 %all-reduce.7.cloned.1.call-start = ((), (), s32[]{:S(2)}) async-start(), calls=%async_computation.9 | async-start | bytes 8388608 | tf_op jit(solution)/shard_map/psum | solution.py:14
  400.9 202.4 %all-gather.9.cloned.1.call-start = ((), (), s32[]{:S(2)}) async-start(), calls=%async_computation.6 | async-start | bytes 2359296 | tf_op jit(solution)/shard_map/all_gather | solution.py:91
  444.8 202.0 %reduce-scatter.5.cloned.1.call-start = ((), (), s32[]{:S(2)}) async-start(), calls=%async_computation.5 | async-start | bytes 2359296 | tf_op jit(solution)/shard_map/reduce_scatter | solution.py:77
  454.9 0.7 copy-start.10
  454.9 1.2 copy-start.11
  454.9 2.5 copy-start.12
  454.9 109.7 %copy-start.2 = (f32[256,256]{1,0:T(8,128)S(1)}, f32[256,256]{1,0:T(8,128)}, u32[]{:S(2)}) copy-start(f32[256,256]{1,0:T(8,128)} %neg.9) | copy-start | bytes 786436
  454.9 191.9 %copy-start.1 = (f32[1,256,256]{2,1,0:T(8,128)S(1)}, f32[1,256,256]{2,1,0:T(8,128)}, u32[]{:S(2)}) copy-start(f32[1,256,256]{2,1,0:T(8,128)} %param.20) | copy-start | bytes 786436
  454.9 490.0 %all-reduce.5.cloned.1.call-start = ((), (), s32[]{:S(2)}) async-start(), calls=%async_computation.8 | async-start | bytes 1572864 | tf_op jit(solution)/shard_map/psum | solution.py:89
  607.7 337.2 %copy-start.6 = (f32[1,256,256]{2,1,0:T(8,128)S(1)}, f32[1,256,256]{2,1,0:T(8,128)}, u32[]{:S(2)}) copy-start(f32[1,256,256]{2,1,0:T(8,128)} %param.15) | copy-start | bytes 786436
  648.4 357.6 %copy-start.4 = (f32[256,256]{1,0:T(8,128)}, f32[256,256]{1,0:T(8,128)S(1)}, u32[]{:S(2)}) copy-start(f32[256,256]{1,0:T(8,128)S(1)} %convolution_subtract_fusion) | copy-start | bytes 786436
  650.6 351.0 %all-gather.11.cloned.1.call-start = ((), (), s32[]{:S(2)}) async-start(), calls=%async_computation.7 | async-start | bytes 2359296 | tf_op jit(solution)/shard_map/all_gather | solution.py:92
  944.9 61.2 %copy-start.9 = (f32[1,256,256]{2,1,0:T(8,128)S(1)}, f32[1,256,256]{2,1,0:T(8,128)}, u32[]{:S(2)}) copy-start(f32[1,256,256]{2,1,0:T(8,128)} %get-tuple-element.8) | copy-start | bytes 786436
  944.9 61.7 %copy-start.7 = (f32[1,256,256]{2,1,0:T(8,128)S(1)}, f32[1,256,256]{2,1,0:T(8,128)}, u32[]{:S(2)}) copy-start(f32[1,256,256]{2,1,0:T(8,128)} %param.21) | copy-start | bytes 786436
  944.9 61.7 %copy-start.8 = (f32[1,256,256]{2,1,0:T(8,128)S(1)}, f32[1,256,256]{2,1,0:T(8,128)}, u32[]{:S(2)}) copy-start(f32[1,256,256]{2,1,0:T(8,128)} %get-tuple-element.9) | copy-start | bytes 786436
  1006.5 1.4 copy-start.3
Sparse Core Ops, SparseCore 0:
  11.9 193.4 all-gather.4
  207.8 189.9 all-gather.6
  400.3 42.7 reduce-scatter.2
  445.7 118.8 all-reduce.6
  566.8 36.3 all-gather.8
  605.7 41.1 reduce-scatter.4
  650.8 294.0 all-reduce.4
  947.5 54.1 all-gather.10
where the time goes:
time: 1020 us; the launch traced here: 1010 us
  waiting for transfers between devices  942 us (92%)
  matrix products  41.9 us (4%)
  between operations  15 us (1%)
  other arithmetic  13.7 us (1%)
    psum x1, waiting for transfers between devices, per_device(): diag_two = dinv_two - lax.psum(part_two, 'pcol')  294 us
    all_gather x1, waiting for transfers between devices, per_device(): rows_two = lax.all_gather(lmat_two, 'pcol', axis=1, tiled=True)  192 us
    all_gather x1, waiting for transfers between devices, per_device(): rows_one = lax.all_gather(lmat_one, 'pcol', axis=1, tiled=True)  179 us
    psum x1, waiting for transfers between devices, broadcast(): return lax.psum(kept, axis)  105 us
    all_gather x1, waiting for transfers between devices, per_device(): lax.all_gather(diag_two, 'prow', axis=0, tiled=True)  55 us
    reduce_scatter x1, waiting for transfers between devices, per_device(): lax.psum_scatter(left_product(rows_two, inverse_anc), 'prow', scatter_dim...  42.2 us
    reduce_scatter x1, waiting for transfers between devices, per_device(): lax.psum_scatter(left_product(rows_one, inverse_anc), 'prow', scatter_dim...  37 us
    all_gather x1, waiting for transfers between devices, per_device(): lax.all_gather(upper_two, 'prow', axis=0, tiled=True)  36.6 us
  transfers between devices with their start and end apart: 8, of which 8 were waited for; matrix products, arithmetic and copies ran while one was open for 4% of the time, Pallas kernels for 0%

commit v1 on v0

v1 whole, which is shorter than its diff:
```python
import functools

import jax
import jax.numpy as jnp
from jax import lax
from jax.experimental import pallas as pl
from jax.experimental.pallas import tpu as pltpu
from jax.sharding import PartitionSpec as P

B = 256
MESH = pl.DeviceIdType.MESH
F32 = jnp.float32
BF16 = jnp.bfloat16
NN = (((1,), (0,)), ((), ()))
NT = (((1,), (1,)), ((), ()))
SEMS = 80


def split(value):
    high = value.astype(BF16)
    return high, (value - high.astype(F32)).astype(BF16)


def mm(left, right, dims=NN):
    lh, ll = split(left)
    rh, rl = split(right)
    dot = functools.partial(lax.dot_general, dimension_numbers=dims, preferred_element_type=F32)
    return dot(lh, rh) + (dot(lh, rl) + dot(ll, rh))


def kernel(
    par, a, lt, lpt, d2, d1,
    u2, u1, g2o, pbo, g1o,
    ag, lg, lh, ll, ah, al, pp, rc, r_in, pl_in, f_in, s_out,
    lloc, lsnd, lpn, d2s, x2all, l2all, x1, red, ry, yr, rz, zr, gz, fin,
    send_sem, recv_sem,
):
    r, q = lax.axis_index("prow"), lax.axis_index("pcol")
    k, c = lax.div(r, 2), lax.rem(r, 2)
    h, y, w = lax.div(q, 8), lax.rem(lax.div(q, 2), 4), lax.rem(q, 2)
    zi = 2 * k + w
    oc = 1 - c
    n = 2 * h + c

    def dev(k=k, c=c, h=h, y=y, w=w):
        return (2 * k + c, 8 * h + 2 * y + w)

    def ring(v, off, size=4):
        return lax.rem(v + (off + size), size)

    def zdev(v):
        return dev(k=lax.div(v, 2), w=lax.rem(v, 2))

    ids = [0]
    pending = []

    def copy(src, dst, device, recv=None, start=True, keep=True):
        num = ids[0]
        ids[0] += 1
        op = pltpu.make_async_remote_copy(
            src_ref=src,
            dst_ref=dst,
            send_sem=send_sem.at[num],
            recv_sem=recv_sem.at[num if recv is None else recv],
            device_id=device,
            device_id_type=MESH,
        )
        if start:
            op.start()
        if keep:
            pending.append(op)
        return op

    barrier = pltpu.get_barrier_semaphore()
    friends = [dev(c=oc)]
    friends += [dev(h=ring(h, o)) for o in (1, 2, 3)]
    friends += [dev(y=ring(y, o)) for o in (1, 2, 3)]
    friends += [zdev(ring(zi, o, 8)) for o in range(1, 8)]
    for friend in friends:
        pl.semaphore_signal(barrier, inc=1, device_id=friend, device_id_type=MESH)

    @pl.when(h != k)
    def _():
        pl.semaphore_signal(barrier, inc=1, device_id=dev(k=h, h=k), device_id_type=MESH)

    pl.semaphore_wait(barrier, len(friends) + jnp.where(h != k, 1, 0))

    hl, hr = dev(h=ring(h, -1)), dev(h=ring(h, 1))
    yl, yr_dev = dev(y=ring(y, -1)), dev(y=ring(y, 1))
    sib = dev(c=oc)
    mine = 2 * y + w
    theirs = 2 * y + 1 - w
    top, bot = pl.ds(0, 512), pl.ds(512, 512)

    lw = copy(lt, lg.at[mine], dev(w=1 - w))
    a_rt = copy(a.at[top], ag.at[0, top], hr)
    a_lb = copy(a.at[bot], ag.at[1, bot], hl)
    l_r0 = copy(lt, lg.at[mine], yr_dev)
    l_l0 = copy(lt, lg.at[mine], yl)
    a_rb = copy(a.at[bot], ag.at[0, bot], hr)
    a_lt = copy(a.at[top], ag.at[1, top], hl)
    lg[mine] = lt[...]
    d2c = copy(d2, d2s, sib)

    lp_recv = ids[0]
    lp_ops = [
        copy(lpt, lpn, dev(k=ring(k, o)), recv=lp_recv, start=False, keep=False) for o in (1, 2, 3)
    ]

    @pl.when(h == k)
    def _():
        lpn[...] = lpt[...]
        for op in lp_ops:
            op.start()

    def split_l(m):
        hi, lo = split(lg[m].reshape(128, 1024))
        lh[m] = hi
        ll[m] = lo

    split_l(mine)
    lw.wait_recv()
    l_r1 = copy(lg.at[theirs], lg.at[theirs], yr_dev)
    l_l1 = copy(lg.at[theirs], lg.at[theirs], yl)
    split_l(theirs)
    a_rt.wait_recv()
    a_fr = copy(ag.at[0, top], ag.at[2, top], hr)
    a_lb.wait_recv()
    a_fl = copy(ag.at[1, bot], ag.at[2, bot], hl)
    from_l, from_r = ring(y, -1), ring(y, 1)
    l_r0.wait_recv()
    m0 = 2 * from_l + w
    l_f0 = copy(lg.at[m0, 0], lg.at[m0, 0], yr_dev)
    l_l0.wait_recv()
    m1 = 2 * from_r + w
    l_f1 = copy(lg.at[m1, 1], lg.at[m1, 1], yl)
    split_l(m0)
    split_l(m1)
    l_r1.wait_recv()
    m2 = 2 * from_l + 1 - w
    l_f2 = copy(lg.at[m2, 0], lg.at[m2, 0], yr_dev)
    l_l1.wait_recv()
    m3 = 2 * from_r + 1 - w
    l_f3 = copy(lg.at[m3, 1], lg.at[m3, 1], yl)
    split_l(m2)
    split_l(m3)
    far = ring(y, 2)
    l_f0.wait_recv()
    l_f1.wait_recv()
    split_l(2 * far + w)
    l_f2.wait_recv()
    l_f3.wait_recv()
    split_l(2 * far + 1 - w)

    cy = lax.div(y, 2)
    off = pl.multiple_of(lax.rem(mine, 4) * B, B)
    l_op = copy(lsnd, lloc, sib, start=False, keep=False)

    @pl.when(c == cy)
    def _():
        for lev in range(2):
            lsnd[lev] = lg[pl.ds(4 * oc, 4), lev, :, pl.ds(off, B)].reshape(B, B)
        l_op.start()
        for lev in range(2):
            lloc[lev] = lg[pl.ds(4 * c, 4), lev, :, pl.ds(off, B)].reshape(B, B)

    @pl.when(c != cy)
    def _():
        l_op.wait_recv()

    def gather_x(buf):
        return [copy(buf.at[n], buf.at[n], dev(h=ring(h, o))) for o in (1, 2, 3)] + [
            copy(buf.at[n], buf.at[n], sib)
        ]

    def gather_sib(buf, ops):
        out = [ops[3]]
        for o in (1, 2, 3):
            ops[o - 1].wait_recv()
            slot = 2 * ring(h, -o) + c
            out.append(copy(buf.at[slot], buf.at[slot], sib))
        return out

    l2all[n] = lloc[0]
    l2_ops = gather_x(l2all)

    def product(parity):
        left_h = lh[pl.ds(4 * parity, 4)].reshape(512, 1024)
        left_l = ll[pl.ds(4 * parity, 4)].reshape(512, 1024)
        dot = functools.partial(lax.dot_general, dimension_numbers=NN, preferred_element_type=F32)
        return dot(left_h, ah[...]) + (dot(left_h, al[...]) + dot(left_l, ah[...]))

    def store(slot, parity, value):
        for quarter in range(4):
            for lev in range(2):
                base = quarter * 128 + lev * 64
                pp[slot, parity, lev, quarter * 64 : quarter * 64 + 64, :] = value[base : base + 64]

    def add_sib(slot, op):
        op.wait_recv()
        for lev in range(2):
            pp[slot, c, lev] += rc[slot, lev]

    blocks = [
        (a, 0, ()),
        (ag.at[0], -1, (a_rb,)),
        (ag.at[1], 1, (a_lt,)),
        (ag.at[2], 2, (a_fr, a_fl)),
    ]
    last = None
    for ref, rel, waits in blocks:
        for op in waits:
            op.wait_recv()
        hi, lo = split(ref[...])
        ah[...] = hi
        al[...] = lo
        slot = ring(h, rel)
        store(slot, oc, product(oc))
        op = copy(pp.at[slot, oc], rc.at[slot], sib)
        store(slot, c, product(c))
        if last is not None:
            add_sib(*last)
        last = (slot, op)
    add_sib(*last)

    kp, km, ko = ring(k, 1), ring(k, -1), ring(k, 2)
    zp, zm = dev(k=kp), dev(k=km)
    up, dn = pl.ds(0, 128), pl.ds(128, 128)
    first = []
    for lev in range(2):
        first.append(
            (
                copy(pp.at[ko, c, lev, up], r_in.at[lev, 0], zp),
                copy(pp.at[ko, c, lev, dn], r_in.at[lev, 1], zm),
                copy(pp.at[kp, c, lev, dn], pl_in.at[lev, 0], zp),
                copy(pp.at[km, c, lev, up], pl_in.at[lev, 1], zm),
            )
        )
    second = []
    for lev in range(2):
        first[lev][0].wait_recv()
        s_out[lev, 0] = r_in[lev, 0] + pp[kp, c, lev, up]
        one = copy(s_out.at[lev, 0], f_in.at[lev, 0], zp)
        first[lev][1].wait_recv()
        s_out[lev, 1] = r_in[lev, 1] + pp[km, c, lev, dn]
        two = copy(s_out.at[lev, 1], f_in.at[lev, 1], zm)
        second.append((one, two))

    l2_sib = gather_sib(l2all, l2_ops)

    def total(lev):
        first[lev][2].wait_recv()
        first[lev][3].wait_recv()
        second[lev][0].wait_recv()
        second[lev][1].wait_recv()
        upper = pp[k, c, lev, up] + f_in[lev, 0] + pl_in[lev, 1]
        lower = pp[k, c, lev, dn] + f_in[lev, 1] + pl_in[lev, 0]
        return jnp.concatenate([upper, lower], axis=0)

    x2all[n] = -total(0)
    x2_ops = gather_x(x2all)
    u2_op = copy(x2all.at[n], u2, dev(k=h, h=k), start=False, keep=False)
    u1_op = copy(x1, u1, dev(k=h, h=k), start=False, keep=False)

    @pl.when(h != k)
    def _():
        u2_op.start()

    @pl.when(h == k)
    def _():
        u2[...] = x2all[n]

    red[0] = mm(lloc[0], x2all[n], NT)
    for op in l2_sib:
        op.wait_recv()

    @pl.when(h != k)
    def _():
        lp_ops[0].wait_recv()

    parent = par[n]
    lp_here = lpn[...]
    l1p = lloc[1] - mm(lp_here, l2all[parent])
    d2c.wait_recv()
    rows = pl.ds(pl.multiple_of(mine * 32, 32), 32)
    here = jnp.where(parent == r, 1.0, 0.0)
    beside = jnp.where(parent == 2 * k + oc, 1.0, 0.0)
    own_rows = mm(d2[rows] * here + d2s[rows] * beside, lp_here, NT)
    main1 = total(1)
    for op in gather_sib(x2all, x2_ops):
        op.wait_recv()
    x2p = x2all[parent]
    x1[...] = -main1 - mm(lp_here, x2p)

    @pl.when(h != k)
    def _():
        u1_op.start()

    @pl.when(h == k)
    def _():
        u1[...] = x1[...]

    red[1] = mm(x2p, l1p, NT)
    red[1, rows] += own_rows
    red[2] = mm(lloc[1], x1[...], NT)

    y_ops = []
    for o in (1, 2, 3):
        to = ring(y, o)
        part = pl.ds(pl.multiple_of(to * 64, 64), 64)
        y_ops.append(copy(red.at[:, part], ry.at[o - 1], dev(y=to)))
    acc = red[:, pl.ds(pl.multiple_of(y * 64, 64), 64), :]
    for o in range(3):
        y_ops[o].wait_recv()
        acc = acc + ry[o]
    yr[...] = acc
    z_ops = []
    for o in range(1, 8):
        to = ring(zi, o, 8)
        part = pl.ds(pl.multiple_of(to * 8, 8), 8)
        z_ops.append(copy(yr.at[:, part], rz.at[o - 1], zdev(to)))
    own = pl.ds(pl.multiple_of(zi * 8, 8), 8)
    acc = yr[:, own, :]
    for o in range(7):
        z_ops[o].wait_recv()
        acc = acc + rz[o]
    zr[...] = acc

    base = ids[0]
    ids[0] += 8
    g_ops = [
        copy(zr, gz.at[:, own], dev(k=h, w=v), recv=base + zi, start=False, keep=False)
        for v in (0, 1)
    ]
    for v in (0, 1):

        @pl.when(2 * h + v != zi)
        def _(v=v):
            g_ops[v].start()

    x_recv = ids[0]
    x_ops = [
        copy(gz, gz, dev(h=ring(h, o)), recv=x_recv, start=False, keep=False) for o in (1, 2, 3)
    ]

    @pl.when(h == k)
    def _():
        gz[:, own, :] = zr[...]
        for o in range(1, 8):
            frm = ring(zi, o, 8)
            pltpu.make_async_remote_copy(
                src_ref=zr,
                dst_ref=gz.at[:, pl.ds(pl.multiple_of(frm * 8, 8), 8)],
                send_sem=send_sem.at[base],
                recv_sem=recv_sem.at[base + frm],
                device_id=sib,
                device_id_type=MESH,
            ).wait_recv()
        for op in x_ops:
            op.start()

    @pl.when(h != k)
    def _():
        x_ops[0].wait_recv()

    part = pl.ds(pl.multiple_of(y * 64, 64), 64)
    f_ops = [copy(gz, fin.at[:, part], dev(y=ring(y, o))) for o in (1, 2, 3)]
    fin[:, part, :] = gz[...]
    for op in f_ops:
        op.wait_recv()
    g2o[...] = d2[...] - fin[0]
    pb = -fin[1]
    pbo[...] = pb
    g1o[...] = d1[...] - fin[2] - mm(lpt[...], pb)

    @pl.when(h != k)
    def _():
        u2_op.wait()
        u1_op.wait()

    @pl.when(h == k)
    def _():
        for op in lp_ops + x_ops:
            op.wait_send()

    @pl.when(c == cy)
    def _():
        l_op.wait_send()

    for v in (0, 1):

        @pl.when(2 * h + v != zi)
        def _(v=v):
            g_ops[v].wait_send()

    for op in pending:
        op.wait_send()
    assert ids[0] <= SEMS


def masked(lower, pattern, widths, row_index, col_index):
    rows_dev, cols_dev = lower.shape
    nblocks = rows_dev // B
    first = col_index * cols_dev
    owner = first // B
    pat = lax.dynamic_slice(pattern, (row_index * nblocks, owner), (nblocks, 1))
    width = lax.dynamic_slice(widths, (owner,), (1,))
    inner = first % B + jnp.arange(cols_dev, dtype=jnp.int32)
    keep = (inner < width).astype(F32)
    block = jnp.repeat(pat[:, 0].astype(F32), B)
    return lower.T * keep[:, None] * block[None, :]


def per_device(
    inverse_anc,
    lower_two,
    pattern_two,
    widths_two,
    dinv_two,
    lower_one,
    pattern_one,
    widths_one,
    parent_one,
    lower_par,
    dinv_one,
):
    row_index = lax.axis_index("prow")
    col_index = lax.axis_index("pcol")
    lt = jnp.stack(
        [
            masked(lower_two, pattern_two, widths_two, row_index, col_index),
            masked(lower_one, pattern_one, widths_one, row_index, col_index),
        ]
    )
    parent = lax.dynamic_slice(parent_one, (row_index,), (1,))
    parent_width = jnp.sum(jnp.where(jnp.arange(8, dtype=jnp.int32) == parent, widths_two, 0))
    own_width = lax.dynamic_slice(widths_one, (row_index,), (1,))
    inner = jnp.arange(B, dtype=jnp.int32)
    lpt = (
        lower_par[0].T
        * (inner[None, :] < parent_width).astype(F32)
        * (inner[:, None] < own_width).astype(F32)
    )
    vmem = pl.BlockSpec(memory_space=pltpu.VMEM)
    square = jax.ShapeDtypeStruct((B, B), F32)
    outs = pl.pallas_call(
        kernel,
        out_shape=[square] * 5,
        in_specs=[pl.BlockSpec(memory_space=pltpu.SMEM)] + [vmem] * 5,
        out_specs=[vmem] * 5,
        scratch_shapes=[
            pltpu.VMEM((3, 1024, B), F32),
            pltpu.VMEM((8, 2, 64, 1024), F32),
            pltpu.VMEM((8, 128, 1024), BF16),
            pltpu.VMEM((8, 128, 1024), BF16),
            pltpu.VMEM((1024, B), BF16),
            pltpu.VMEM((1024, B), BF16),
            pltpu.VMEM((4, 2, 2, B, B), F32),
            pltpu.VMEM((4, 2, B, B), F32),
            pltpu.VMEM((2, 2, 128, B), F32),
            pltpu.VMEM((2, 2, 128, B), F32),
            pltpu.VMEM((2, 2, 128, B), F32),
            pltpu.VMEM((2, 2, 128, B), F32),
            pltpu.VMEM((2, B, B), F32),
            pltpu.VMEM((2, B, B), F32),
            pltpu.VMEM((B, B), F32),
            pltpu.VMEM((B, B), F32),
            pltpu.VMEM((8, B, B), F32),
            pltpu.VMEM((8, B, B), F32),
            pltpu.VMEM((B, B), F32),
            pltpu.VMEM((3, B, B), F32),
            pltpu.VMEM((3, 3, 64, B), F32),
            pltpu.VMEM((3, 64, B), F32),
            pltpu.VMEM((7, 3, 8, B), F32),
            pltpu.VMEM((3, 8, B), F32),
            pltpu.VMEM((3, 64, B), F32),
            pltpu.VMEM((3, B, B), F32),
            pltpu.SemaphoreType.DMA((SEMS,)),
            pltpu.SemaphoreType.DMA((SEMS,)),
        ],
        compiler_params=pltpu.CompilerParams(
            collective_id=0, has_side_effects=True, vmem_limit_bytes=56 * 1024 * 1024
        ),
    )(parent_one, inverse_anc, lt, lpt, dinv_two[0], dinv_one[0])
    u2, u1, g2, pb, g1 = outs
    return u2, g2[None], u1, pb[None], g1[None]


def solution(mesh):
    in_specs = (
        P("prow", "pcol"),
        P("prow", "pcol"),
        P(),
        P(),
        P("prow", None, None),
        P("prow", "pcol"),
        P(),
        P(),
        P(),
        P("prow", None, None),
        P("prow", None, None),
    )
    out_specs = (
        P("prow", "pcol"),
        P("prow", None, None),
        P("prow", "pcol"),
        P("prow", None, None),
        P("prow", None, None),
    )
    return jax.shard_map(
        per_device, mesh=mesh, in_specs=in_specs, out_specs=out_specs, check_vma=False
    )
```

time: 1020 us -> 202 us (0.20)
  the two profiles are of different devices: /device:TPU:4 before, /device:TPU:128 now
where the time goes in v1:
time: 202 us; the launch traced here: 201 us
  Pallas kernels  183 us (91%)
  local copies, waits for them, and re-layouts  9.71 us (5%)
  other arithmetic  7.45 us (4%)
    pallas_call x1, Pallas kernels, per_device(): pl.pallas_call(kernel, out_shape=[square] * 5, in_specs=[pl.BlockSpec(mem...  183 us
    unnamed x28, local copies, waits for them, and re-layouts  7.96 us

profile of v1, /device:TPU:128, one launch (start us, length us, event | category | flops | bytes accessed | tf_op | source)
XLA Modules:
  0.0 201.1 jit_solution(438868623396200671)
XLA Ops:
  0.7 0.0 copy-start.7
  0.7 0.6 copy-done.7
  1.3 0.6 dynamic_slice.22
  1.9 0.7 copy-done.8
  2.6 1.3 fusion.2
  3.8 0.6 dynamic_slice.18
  4.4 0.8 convert_bitcast_fusion
  5.2 0.7 copy-done.6
  5.8 0.6 fusion.3
  6.4 1.3 compare_convert_fusion.2
  7.7 1.3 compare_convert_fusion
  9.0 0.1 broadcast_bitcast_fusion
  9.1 0.1 broadcast_bitcast_fusion.1
  9.2 1.1 multiply_bitcast_fusion.1
  10.3 0.0 copy-done
  10.3 0.1 multiply_bitcast_fusion
  10.4 0.0 copy-start.1
  10.4 0.8 pad_maximum_fusion.lt
  11.2 0.2 copy-done.1
  11.4 0.1 copy.16
  11.5 0.8 fusion.1.lpt
  12.3 183.2 %shard_map.146 = (f32[256,256]{1,0:T(8,128)}, f32[256,256]{1,0:T(8,128)}, f32[256,256]{1,0:T(8,128)}, f32[256,256]{1,0:T(8,128)}, f32[256,256]{1,0:T(8,128)}) custom-call(s32[8]{0:T(128)} %par.1, f32[1024,256]{1,0:T(8,128)} %a.1, f32[2,64,1024]{2,1,0:T(8,128)} %pad_maximum_fusion.lt, f32[256,256]{1,0:T(8,128)} %fusion.1.lpt, f32[256,256]{1,0:T(8,128)} %bitcast.35, ...), custom_call_target="tpu_custom_call" | custom-call | tf_op jit(solution)/shard_map/pallas_call | solution.py:446
  195.6 0.0 copy-start.5
  195.6 1.7 copy.24
  197.3 0.0 copy-done.5
  197.3 0.7 copy.25
  198.0 0.3 copy-done.4
  198.3 0.7 copy.26
  199.0 0.3 copy-done.3
  199.4 0.7 copy.27
  200.1 0.3 copy-done.2
  200.4 0.7 copy.28
  (8 shorter events, 0.0 us)
Async XLA Ops:
  0.7 0.7 copy-start.7
  1.9 0.7 copy-start.8
  5.2 0.7 copy-start.6
  9.2 1.1 copy-start
  10.4 1.0 copy-start.1
  195.6 1.7 copy-start.5
  197.3 1.0 copy-start.4
  198.3 1.0 copy-start.3
  199.4 1.0 copy-start.2

commit v2 on v0

v2 whole, which is shorter than its diff:
```python
import functools

import jax
import jax.numpy as jnp
from jax import lax
from jax.experimental import pallas as pl
from jax.experimental.pallas import tpu as pltpu
from jax.sharding import PartitionSpec as P

B = 256
MESH = pl.DeviceIdType.MESH
F32 = jnp.float32
BF16 = jnp.bfloat16
NN = (((1,), (0,)), ((), ()))
NT = (((1,), (1,)), ((), ()))
SEMS = 160


def split(value):
    high = value.astype(BF16)
    return high, (value - high.astype(F32)).astype(BF16)


def dot3(lh, ll, rh, rl, dims=NN):
    dot = functools.partial(lax.dot_general, dimension_numbers=dims, preferred_element_type=F32)
    return dot(lh, rh) + (dot(lh, rl) + dot(ll, rh))


def mm(left, right, dims=NN):
    return dot3(*split(left), *split(right), dims)


def kernel(
    par, wid2, wid1, pat2, pat1, a, low2, low1, lpar, d2, d1,
    u2, u1, g2o, pbo, g1o,
    ag, lt, lg, lh, ll, ah, al, pp, rc, r_in, pl_in, f_in, s_out,
    lloc, lsnd, lpt, lpn, d2s, x2all, l2all, x1, t_z, t_x,
    red_a, ry_a, yr_a, rz_a, zr_a, gz_a, fin_a,
    red_b, ry_b, yr_b, rz_b, zr_b, gz_b, fin_b,
    send_sem, recv_sem,
):
    r, q = lax.axis_index("prow"), lax.axis_index("pcol")
    k, c = lax.div(r, 2), lax.rem(r, 2)
    h, y, w = lax.div(q, 8), lax.rem(lax.div(q, 2), 4), lax.rem(q, 2)
    zi = 2 * k + w
    oc = 1 - c
    n = 2 * h + c

    def dev(k=k, c=c, h=h, y=y, w=w):
        return (2 * k + c, 8 * h + 2 * y + w)

    def ring(v, off, size=4):
        return lax.rem(v + (off + size), size)

    def zdev(v):
        return dev(k=lax.div(v, 2), w=lax.rem(v, 2))

    ids = [0]
    pending = []

    def take(count):
        ids[0] += count
        return ids[0] - count

    def copy(src, dst, device, recv=None, start=True):
        num = take(1)
        op = pltpu.make_async_remote_copy(
            src_ref=src,
            dst_ref=dst,
            send_sem=send_sem.at[num],
            recv_sem=recv_sem.at[num if recv is None else recv],
            device_id=device,
            device_id_type=MESH,
        )
        if start:
            op.start()
            pending.append(op)
        return op

    def arrival(dst, recv):
        return pltpu.make_async_remote_copy(
            src_ref=dst,
            dst_ref=dst,
            send_sem=send_sem.at[0],
            recv_sem=recv_sem.at[recv],
            device_id=dev(c=oc),
            device_id_type=MESH,
        )

    barrier = pltpu.get_barrier_semaphore()
    friends = [dev(c=oc)]
    friends += [dev(h=ring(h, o)) for o in (1, 2, 3)]
    friends += [dev(y=ring(y, o)) for o in (1, 2, 3)]
    friends += [zdev(ring(zi, o, 8)) for o in range(1, 8)]
    for friend in friends:
        pl.semaphore_signal(barrier, inc=1, device_id=friend, device_id_type=MESH)

    owner = lax.div(q, 4)
    inner = lax.rem(q, 4) * 64 + lax.broadcasted_iota(jnp.int32, (64, 1024), 0)
    block = lax.broadcasted_iota(jnp.int32, (64, 1024), 1) // B
    for lev, (low, pat, wid) in enumerate(((low2, pat2, wid2), (low1, pat1, wid1))):
        present = jnp.zeros((64, 1024), F32)
        for b in range(4):
            there = pat[4 * r + b, owner].astype(F32)
            present = jnp.where(block == b, there, present)
        keep = jnp.where(inner < wid[owner], present, 0.0)
        lt[lev] = low[...].T * keep
    row = lax.broadcasted_iota(jnp.int32, (B, B), 0)
    col = lax.broadcasted_iota(jnp.int32, (B, B), 1)
    inside = jnp.where(row < wid1[r], 1.0, 0.0) * jnp.where(col < wid2[par[r]], 1.0, 0.0)
    lpt[...] = lpar[0].T * inside

    pl.semaphore_wait(barrier, len(friends))

    hl, hr = dev(h=ring(h, -1)), dev(h=ring(h, 1))
    yl, yr = dev(y=ring(y, -1)), dev(y=ring(y, 1))
    sib, pair = dev(c=oc), dev(w=1 - w)
    mine = 2 * y + w
    theirs = 2 * y + 1 - w
    ml, mr, mf = 2 * ring(y, -1), 2 * ring(y, 1), 2 * ring(y, 2)
    top, bot = pl.ds(0, 512), pl.ds(512, 512)

    def split_l(lev, m):
        hi, lo = split(lg[lev, m])
        lh[lev, m] = hi
        ll[lev, m] = lo

    def send_own(lev):
        return (
            copy(lt.at[lev], lg.at[lev, mine], yr),
            copy(lt.at[lev], lg.at[lev, mine], yl),
        )

    def send_pair(lev):
        return (
            copy(lg.at[lev, theirs], lg.at[lev, theirs], yr),
            copy(lg.at[lev, theirs], lg.at[lev, theirs], yl),
        )

    def forward_l(lev, ops, which):
        near, far = pl.ds(0, 32), pl.ds(32, 32)
        ops[0].wait_recv()
        one = copy(lg.at[lev, ml + which, near], lg.at[lev, ml + which, near], yr)
        ops[1].wait_recv()
        two = copy(lg.at[lev, mr + which, far], lg.at[lev, mr + which, far], yl)
        return one, two

    w2 = copy(lt.at[0], lg.at[0, mine], pair)
    o2 = send_own(0)
    a_rt = copy(a.at[top], ag.at[0, top], hr)
    a_lb = copy(a.at[bot], ag.at[1, bot], hl)
    a_rb = copy(a.at[bot], ag.at[0, bot], hr)
    a_lt = copy(a.at[top], ag.at[1, top], hl)
    d2c = copy(d2, d2s, sib)
    lg[0, mine] = lt[0]
    lg[1, mine] = lt[1]
    split_l(0, mine)
    split_l(1, mine)

    def split_a(ref, slot):
        hi, lo = split(ref[...])
        ah[slot] = hi
        al[slot] = lo

    split_a(a, 0)
    w2.wait_recv()
    p2 = send_pair(0)
    w1 = copy(lt.at[1], lg.at[1, mine], pair)
    f2 = forward_l(0, o2, w)
    split_l(0, theirs)
    split_l(0, ml + w)
    split_l(0, mr + w)
    a_rt.wait_recv()
    a_fr = copy(ag.at[0, top], ag.at[2, top], hr)
    a_lb.wait_recv()
    a_fl = copy(ag.at[1, bot], ag.at[2, bot], hl)
    e2 = forward_l(0, p2, 1 - w)
    o1 = send_own(1)
    split_l(0, ml + 1 - w)
    split_l(0, mr + 1 - w)

    lp_recv = ids[0]
    lp_ops = [copy(lpt, lpn, dev(k=ring(k, o)), recv=lp_recv, start=False) for o in (1, 2, 3)]

    @pl.when(h == k)
    def _():
        lpn[...] = lpt[...]
        for op in lp_ops:
            op.start()

    for op in f2:
        op.wait_recv()
    split_l(0, mf + w)
    w1.wait_recv()
    p1 = send_pair(1)
    split_l(1, theirs)
    for op in e2:
        op.wait_recv()
    split_l(0, mf + 1 - w)

    cy = lax.div(y, 2)
    off = pl.multiple_of(lax.rem(mine, 4) * B, B)
    l_ops = [copy(lsnd.at[lev], lloc.at[lev], sib, start=False) for lev in range(2)]

    def share(lev):
        @pl.when(c == cy)
        def _():
            lsnd[lev] = lg[lev, pl.ds(4 * oc, 4), :, pl.ds(off, B)].reshape(B, B)
            l_ops[lev].start()
            lloc[lev] = lg[lev, pl.ds(4 * c, 4), :, pl.ds(off, B)].reshape(B, B)

        @pl.when(c != cy)
        def _():
            l_ops[lev].wait_recv()

    kp, km, ko = ring(k, 1), ring(k, -1), ring(k, 2)
    zp, zm = dev(k=kp), dev(k=km)
    up, dn = pl.ds(0, 128), pl.ds(128, 128)
    rs = [
        (
            copy(pp.at[ko, lev, c, up], r_in.at[lev, 0], zp, start=False),
            copy(pp.at[ko, lev, c, dn], r_in.at[lev, 1], zm, start=False),
            copy(pp.at[kp, lev, c, dn], pl_in.at[lev, 0], zp, start=False),
            copy(pp.at[km, lev, c, up], pl_in.at[lev, 1], zm, start=False),
            copy(s_out.at[lev, 0], f_in.at[lev, 0], zp, start=False),
            copy(s_out.at[lev, 1], f_in.at[lev, 1], zm, start=False),
        )
        for lev in range(2)
    ]

    def product(lev, slot, block):
        def half(parity):
            left_h = lh[lev, pl.ds(4 * parity, 4)].reshape(B, 1024)
            left_l = ll[lev, pl.ds(4 * parity, 4)].reshape(B, 1024)
            pp[slot, lev, parity] = dot3(left_h, left_l, ah[block], al[block])

        half(oc)
        op = copy(pp.at[slot, lev, oc], rc.at[slot, lev], sib)
        half(c)
        op.wait_recv()
        pp[slot, lev, c] += rc[slot, lev]
        role = ring(slot, 4 - k)

        @pl.when(role == 2)
        def _():
            rs[lev][0].start()
            rs[lev][1].start()

        @pl.when(role == 1)
        def _():
            rs[lev][2].start()

        @pl.when(role == 3)
        def _():
            rs[lev][3].start()

    def relay(lev, slot):
        role = ring(slot, 4 - k)

        @pl.when(role == 1)
        def _():
            rs[lev][0].wait_recv()
            s_out[lev, 0] = r_in[lev, 0] + pp[slot, lev, c, up]
            rs[lev][4].start()

        @pl.when(role == 3)
        def _():
            rs[lev][1].wait_recv()
            s_out[lev, 1] = r_in[lev, 1] + pp[slot, lev, c, dn]
            rs[lev][5].start()

    s0, s1, s2, s3 = h, ring(h, -1), ring(h, 1), ring(h, 2)
    product(0, s0, 0)
    share(0)
    f1 = forward_l(1, o1, w)
    split_l(1, ml + w)
    split_l(1, mr + w)
    relay(0, s0)
    a_rb.wait_recv()
    split_a(ag.at[0], 1)
    product(0, s1, 1)
    e1 = forward_l(1, p1, 1 - w)
    split_l(1, ml + 1 - w)
    split_l(1, mr + 1 - w)
    a_lt.wait_recv()
    split_a(ag.at[1], 2)
    product(0, s2, 2)
    relay(0, s1)
    for op in f1:
        op.wait_recv()
    split_l(1, mf + w)
    for op in e1:
        op.wait_recv()
    split_l(1, mf + 1 - w)
    a_fr.wait_recv()
    a_fl.wait_recv()
    split_a(ag.at[2], 3)
    product(0, s3, 3)
    relay(0, s2)

    def gather_start(buf):
        return copy(buf.at[n], buf.at[n], hr), copy(buf.at[n], buf.at[n], hl), copy(
            buf.at[n], buf.at[n], sib
        )

    def gather_mid(buf, ops):
        left, right = 2 * ring(h, -1) + c, 2 * ring(h, 1) + c
        ops[0].wait_recv()
        one = copy(buf.at[left, up], buf.at[left, up], hr)
        sib_l = copy(buf.at[left], buf.at[left], sib)
        ops[1].wait_recv()
        two = copy(buf.at[right, dn], buf.at[right, dn], hl)
        sib_r = copy(buf.at[right], buf.at[right], sib)
        return one, two, ops[2], sib_l, sib_r

    def gather_end(buf, ops):
        opp = 2 * ring(h, 2) + c
        ops[0].wait_recv()
        ops[1].wait_recv()
        last = copy(buf.at[opp], buf.at[opp], sib)
        for op in ops[2:]:
            op.wait_recv()
        last.wait_recv()

    l2all[n] = lloc[0]
    lx = gather_start(l2all)
    product(1, s0, 0)
    relay(0, s3)
    share(1)
    product(1, s1, 1)
    relay(1, s0)
    lx = gather_mid(l2all, lx)
    product(1, s2, 2)
    relay(1, s1)
    product(1, s3, 3)
    relay(1, s2)
    gather_end(l2all, lx)

    def total(lev):
        for op in rs[lev][2:]:
            op.wait_recv()
        upper = pp[k, lev, c, up] + f_in[lev, 0] + pl_in[lev, 1]
        lower = pp[k, lev, c, dn] + f_in[lev, 1] + pl_in[lev, 0]
        return jnp.concatenate([upper, lower], axis=0)

    def place(lev, buf, out):
        z_base, x_base = take(4), take(4)
        via_z = copy(
            buf.at[up], t_z.at[lev, k], dev(k=h), recv=z_base + ring(k, 4 - h), start=False
        )
        via_x = copy(
            buf.at[dn], t_x.at[lev, h], dev(h=k), recv=x_base + ring(h, 4 - k), start=False
        )
        got_z, got_x = ids[0], ids[0] + 1
        take(2)
        on = []
        for o in (1, 2, 3):
            v = ring(k, o)
            on.append(copy(t_z.at[lev, v], out.at[up], dev(h=v), recv=got_z, start=False))
            on.append(copy(t_x.at[lev, v], out.at[dn], dev(k=v), recv=got_x, start=False))

        @pl.when(h != k)
        def _():
            via_z.start()
            via_x.start()

        @pl.when(h == k)
        def _():
            out[...] = buf[...]

        def pass_on():
            @pl.when(h == k)
            def _():
                for o in (1, 2, 3):
                    v = ring(k, o)
                    arrival(t_z.at[lev, v], z_base + o).wait_recv()
                    on[2 * o - 2].start()
                    arrival(t_x.at[lev, v], x_base + o).wait_recv()
                    on[2 * o - 1].start()

        def finish():
            @pl.when(h != k)
            def _():
                via_z.wait_send()
                via_x.wait_send()
                arrival(out.at[up], got_z).wait_recv()
                arrival(out.at[dn], got_x).wait_recv()

            @pl.when(h == k)
            def _():
                for op in on:
                    op.wait_send()

        return pass_on, finish

    x2all[n] = -total(0)
    xx = gather_start(x2all)
    relay(1, s3)
    pass_2, finish_2 = place(0, x2all.at[n], u2)
    red_a[0] = mm(lloc[0], x2all[n], NT)

    @pl.when(h != k)
    def _():
        lp_ops[0].wait_recv()

    parent = par[n]
    lp_h, lp_l = split(lpn[...])
    l1p = lloc[1] - dot3(lp_h, lp_l, *split(l2all[parent]))
    d2c.wait_recv()
    rows = pl.ds(pl.multiple_of(mine * 32, 32), 32)
    here = jnp.where(parent == r, 1.0, 0.0)
    beside = jnp.where(parent == 2 * k + oc, 1.0, 0.0)
    own_rows = dot3(*split(d2[0, rows] * here + d2s[0, rows] * beside), lp_h, lp_l, NT)
    xx = gather_mid(x2all, xx)
    pass_2()
    gather_end(x2all, xx)
    x2p = x2all[parent]
    red_a[1] = mm(x2p, l1p, NT)
    red_a[1, rows] += own_rows

    own8 = pl.ds(pl.multiple_of(zi * 8, 8), 8)
    own64 = pl.ds(pl.multiple_of(y * 64, 64), 64)

    class Chain:
        def __init__(self, red, ry, yr, rz, zr, gz, fin):
            self.bufs = (red, ry, yr, rz, zr, gz, fin)

        def y_start(self):
            red, ry = self.bufs[:2]
            self.ops = []
            for o in (1, 2, 3):
                to = ring(y, o)
                part = pl.ds(pl.multiple_of(to * 64, 64), 64)
                self.ops.append(copy(red.at[:, part], ry.at[o - 1], dev(y=to)))

        def z_start(self):
            red, ry, yr, rz = self.bufs[:4]
            acc = red[:, own64, :]
            for o in range(3):
                self.ops[o].wait_recv()
                acc = acc + ry[o]
            yr[...] = acc
            self.ops = []
            for o in range(1, 8):
                to = ring(zi, o, 8)
                part = pl.ds(pl.multiple_of(to * 8, 8), 8)
                self.ops.append(copy(yr.at[:, part], rz.at[o - 1], zdev(to)))

        def plane_start(self):
            yr, rz, zr, gz = self.bufs[2:6]
            acc = yr[:, own8, :]
            for o in range(7):
                self.ops[o].wait_recv()
                acc = acc + rz[o]
            zr[...] = acc
            self.base = take(8)
            self.sends = []
            for v in (0, 1):
                op = copy(
                    zr, gz.at[:, own8], dev(k=h, w=v), recv=self.base + zi, start=False
                )
                self.sends.append(op)

                @pl.when(2 * h + v != zi)
                def _(op=op):
                    op.start()

        def x_spread(self):
            zr, gz = self.bufs[4:6]
            got = ids[0]
            self.spread = [
                copy(gz, gz, dev(h=ring(h, o)), recv=got, start=False) for o in (1, 2, 3)
            ]

            @pl.when(h == k)
            def _():
                gz[:, own8, :] = zr[...]
                for o in range(1, 8):
                    frm = ring(zi, o, 8)
                    part = pl.ds(pl.multiple_of(frm * 8, 8), 8)
                    arrival(gz.at[:, part], self.base + frm).wait_recv()
                for op in self.spread:
                    op.start()

            @pl.when(h != k)
            def _():
                self.spread[0].wait_recv()

        def y_spread(self):
            gz, fin = self.bufs[5:]
            self.ops = [copy(gz, fin.at[:, own64], dev(y=ring(y, o))) for o in (1, 2, 3)]
            fin[:, own64, :] = gz[...]

        def finish(self):
            for op in self.ops:
                op.wait_recv()

        def drain(self):
            for v in (0, 1):

                @pl.when(2 * h + v != zi)
                def _(v=v):
                    self.sends[v].wait_send()

            @pl.when(h == k)
            def _():
                for op in self.spread:
                    op.wait_send()

    first = Chain(red_a, ry_a, yr_a, rz_a, zr_a, gz_a, fin_a)
    second = Chain(red_b, ry_b, yr_b, rz_b, zr_b, gz_b, fin_b)
    first.y_start()
    correction = dot3(lp_h, lp_l, *split(x2p))
    x1[...] = -total(1) - correction
    pass_1, finish_1 = place(1, x1, u1)
    red_b[0] = mm(lloc[1], x1[...], NT)
    second.y_start()
    first.z_start()
    second.z_start()
    first.plane_start()
    second.plane_start()
    pass_1()
    first.x_spread()
    first.y_spread()
    second.x_spread()
    second.y_spread()
    first.finish()
    g2o[...] = d2[0] - fin_a[0]
    pb = -fin_a[1]
    pbo[...] = pb
    update = d1[0] - mm(lpt[...], pb)
    second.finish()
    g1o[...] = update - fin_b[0]
    finish_2()
    finish_1()
    first.drain()
    second.drain()

    @pl.when(h == k)
    def _():
        for op in lp_ops:
            op.wait_send()

    @pl.when(c == cy)
    def _():
        for op in l_ops:
            op.wait_send()

    for lev in range(2):
        for op in rs[lev]:
            op.wait_send()
    for op in pending:
        op.wait_send()
    assert ids[0] <= SEMS


def settle(*refs):
    for src, dst in zip(refs[:5], refs[5:]):
        dst[...] = src[...].reshape(dst.shape)


def per_device(
    inverse_anc,
    lower_two,
    pattern_two,
    widths_two,
    dinv_two,
    lower_one,
    pattern_one,
    widths_one,
    parent_one,
    lower_par,
    dinv_one,
):
    vmem = pl.BlockSpec(memory_space=pltpu.VMEM)
    smem = pl.BlockSpec(memory_space=pltpu.SMEM)
    square = jax.ShapeDtypeStruct((B, B), F32)
    cube = jax.ShapeDtypeStruct((1, B, B), F32)

    def chain(count):
        return [
            pltpu.VMEM((count, B, B), F32),
            pltpu.VMEM((3, count, 64, B), F32),
            pltpu.VMEM((count, 64, B), F32),
            pltpu.VMEM((7, count, 8, B), F32),
            pltpu.VMEM((count, 8, B), F32),
            pltpu.VMEM((count, 64, B), F32),
            pltpu.VMEM((count, B, B), F32),
        ]

    outs = pl.pallas_call(
        kernel,
        out_shape=[square] * 5,
        in_specs=[smem] * 5 + [vmem] * 6,
        out_specs=[vmem] * 5,
        scratch_shapes=[
            pltpu.VMEM((3, 1024, B), F32),
            pltpu.VMEM((2, 64, 1024), F32),
            pltpu.VMEM((2, 8, 64, 1024), F32),
            pltpu.VMEM((2, 8, 64, 1024), BF16),
            pltpu.VMEM((2, 8, 64, 1024), BF16),
            pltpu.VMEM((4, 1024, B), BF16),
            pltpu.VMEM((4, 1024, B), BF16),
            pltpu.VMEM((4, 2, 2, B, B), F32),
            pltpu.VMEM((4, 2, B, B), F32),
            pltpu.VMEM((2, 2, 128, B), F32),
            pltpu.VMEM((2, 2, 128, B), F32),
            pltpu.VMEM((2, 2, 128, B), F32),
            pltpu.VMEM((2, 2, 128, B), F32),
            pltpu.VMEM((2, B, B), F32),
            pltpu.VMEM((2, B, B), F32),
            pltpu.VMEM((B, B), F32),
            pltpu.VMEM((B, B), F32),
            pltpu.VMEM((1, B, B), F32),
            pltpu.VMEM((8, B, B), F32),
            pltpu.VMEM((8, B, B), F32),
            pltpu.VMEM((B, B), F32),
            pltpu.VMEM((2, 4, 128, B), F32),
            pltpu.VMEM((2, 4, 128, B), F32),
            *chain(2),
            *chain(1),
            pltpu.SemaphoreType.DMA((SEMS,)),
            pltpu.SemaphoreType.DMA((SEMS,)),
        ],
        compiler_params=pltpu.CompilerParams(
            collective_id=0, has_side_effects=True, vmem_limit_bytes=56 * 1024 * 1024
        ),
    )(
        parent_one,
        widths_two,
        widths_one,
        pattern_two,
        pattern_one,
        inverse_anc,
        lower_two,
        lower_one,
        lower_par,
        dinv_two,
        dinv_one,
    )
    u2, g2, u1, pb, g1 = pl.pallas_call(
        settle,
        out_shape=[square, cube, square, cube, cube],
        in_specs=[vmem] * 5,
        out_specs=[vmem] * 5,
    )(outs[0], outs[2], outs[1], outs[3], outs[4])
    return u2, g2, u1, pb, g1


def solution(mesh):
    in_specs = (
        P("prow", "pcol"),
        P("prow", "pcol"),
        P(),
        P(),
        P("prow", None, None),
        P("prow", "pcol"),
        P(),
        P(),
        P(),
        P("prow", None, None),
        P("prow", None, None),
    )
    out_specs = (
        P("prow", "pcol"),
        P("prow", None, None),
        P("prow", "pcol"),
        P("prow", None, None),
        P("prow", None, None),
    )
    return jax.shard_map(
        per_device, mesh=mesh, in_specs=in_specs, out_specs=out_specs, check_vma=False
    )
```

time: 1020 us -> 151 us (0.15)
  waiting for transfers between devices: 942 us -> 0 us
  Pallas kernels: 0 us -> 143 us
  matrix products: 41.9 us -> 0 us
  between operations: 15 us -> 0.65 us
  other arithmetic: 13.7 us -> 0 us
    all_gather x4 -> x0, waiting for transfers between devices: 463 us -> none  [the longest x1 192 us: per_device(): rows_two = lax.all_gather(lmat_two, 'pcol', axis=1, tiled=True)]
    psum x2 -> x0, waiting for transfers between devices: 399 us -> none  [the longest x1 294 us: per_device(): diag_two = dinv_two - lax.psum(part_two, 'pcol')]
    pallas_call x0 -> x2, Pallas kernels: none -> 143 us  [the longest x1 141 us: per_device(): pl.pallas_call(kernel, out_shape=[square] * 5, in_specs=[smem] * 5 + [vme...]
    reduce_scatter x2 -> x0, waiting for transfers between devices: 79.2 us -> none  [the longest x1 42.2 us: per_device(): lax.psum_scatter(left_product(rows_two, inverse_anc), 'prow', scatter_dim...]
    dot_general x12 -> x0, matrix products: 41.9 us -> none  [the longest x2 20 us: left_product(): lax.dot_general(piece, inverse_anc, (((0,), (0,)), ((), ())), precision=H...]
  transfers between devices with their start and end apart: 8 -> 0, of which waited for: 8 -> 0; matrix products, arithmetic and copies ran while one was open for 4% -> 0% of each run, Pallas kernels for 0% -> 0%
where the time goes in v2:
time: 151 us; the launch traced here: 149 us
  Pallas kernels  143 us (95%)
  local copies, waits for them, and re-layouts  5.05 us (3%)
    pallas_call x1, Pallas kernels, per_device(): pl.pallas_call(kernel, out_shape=[square] * 5, in_specs=[smem] * 5 + [vme...  141 us
    unnamed x8, local copies, waits for them, and re-layouts  5.05 us

profile of v2, /device:TPU:4, one launch (start us, length us, event | category | flops | bytes accessed | tf_op | source)
XLA Modules:
  0.0 149.0 jit_solution(9325344237339317568)
XLA Ops:
  0.6 0.0 copy-start.1
  0.6 1.4 copy.16.pat2
  2.0 0.0 copy-done.1
  2.0 0.7 copy.17.pat1
  2.7 0.0 copy-start
  2.7 2.0 %copy.18.low2 = f32[1024,64]{1,0:T(8,128)} copy(f32[1024,64]{0,1:T(8,128)} %param.12) | data formatting | bytes 524288 | tf_op args[1]
  4.7 0.0 copy-done
  4.7 1.0 copy.19.low1
  5.7 141.0 %shard_map.146 = (f32[256,256]{1,0:T(8,128)}, f32[256,256]{1,0:T(8,128)}, f32[256,256]{1,0:T(8,128)}, f32[256,256]{1,0:T(8,128)}, f32[256,256]{1,0:T(8,128)}) custom-call(s32[8]{0:T(128)} %par.1, s32[8]{0:T(128)} %wid2.1, s32[8]{0:T(128)} %wid1.1, s32[32,8]{1,0:T(8,128)} %copy.16.pat2, s32[32,8]{1,0:T(8,128)} %copy.17.pat1, f32[1024,256]{1,0:T(8,128)} %a.1, ...), custom_call_target="tpu_custom_call" | custom-call | tf_op jit(solution)/shard_map/pallas_call | solution.py:591
  146.7 2.3 %shard_map.147 = (f32[256,256]{1,0:T(8,128)}, f32[1,256,256]{2,1,0:T(8,128)}, f32[256,256]{1,0:T(8,128)}, f32[1,256,256]{2,1,0:T(8,128)}, f32[1,256,256]{2,1,0:T(8,128)}) custom-call(f32[256,256]{1,0:T(8,128)} %get-tuple-element.10.refs_0_, f32[256,256]{1,0:T(8,128)} %get-tuple-element.11.refs_1_, f32[256,256]{1,0:T(8,128)} %get-tuple-element.12.refs_2_, ...), custom_call_target="tpu_custom_call" | custom-call | tf_op jit(solution)/shard_map/pallas_call | solution.py:641
Async XLA Ops:
  0.6 1.4 copy-start.1
  2.7 2.0 %copy-start = (f32[1024,64]{0,1:T(8,128)S(1)}, f32[1024,64]{0,1:T(8,128)}, u32[]{:S(2)}) copy-start(f32[1024,64]{0,1:T(8,128)} %param.16) | copy-start | bytes 786436

commit v3 on v2

v3 whole, which is shorter than its diff:
```python
import functools

import jax
import jax.numpy as jnp
from jax import lax
from jax.experimental import pallas as pl
from jax.experimental.pallas import tpu as pltpu
from jax.sharding import PartitionSpec as P

B = 256
MESH = pl.DeviceIdType.MESH
F32 = jnp.float32
BF16 = jnp.bfloat16
NN = (((1,), (0,)), ((), ()))
NT = (((1,), (1,)), ((), ()))
SEMS = 300


def split(value):
    high = value.astype(BF16)
    return high, (value - high.astype(F32)).astype(BF16)


def dot3(lh, ll, rh, rl, dims=NN):
    dot = functools.partial(lax.dot_general, dimension_numbers=dims, preferred_element_type=F32)
    return dot(lh, rh) + (dot(lh, rl) + dot(ll, rh))


def mm(left, right, dims=NN):
    return dot3(*split(left), *split(right), dims)


def kernel(
    par, wid2, wid1, pat2, pat1, a, low2, low1, lpar, d2, d1,
    u2, u1, g2o, pbo, g1o,
    ag, lt, lg, lh, ll, ah, al, pp, rc, r_in, pl_in, f_in, s_out,
    lloc, lsnd, lpt, lpn, d2s, x2all, x2, x1, t_z, t_x, g_all,
    red_g, ry_g, yr_g, rz_g, zr_g, gz_g, fin_g,
    red_f, ry_f, yr_f, rz_f, zr_f, gz_f, fin_f,
    red_s, ry_s, yr_s, rz_s, zr_s, gz_s, fin_s,
    send_sem, recv_sem,
):
    r, q = lax.axis_index("prow"), lax.axis_index("pcol")
    k, c = lax.div(r, 2), lax.rem(r, 2)
    h, y, w = lax.div(q, 8), lax.rem(lax.div(q, 2), 4), lax.rem(q, 2)
    zi = 2 * k + w
    oc = 1 - c
    n = 2 * h + c

    def dev(k=k, c=c, h=h, y=y, w=w):
        return (2 * k + c, 8 * h + 2 * y + w)

    def ring(v, off, size=4):
        return lax.rem(v + (off + size), size)

    def zdev(v):
        return dev(k=lax.div(v, 2), w=lax.rem(v, 2))

    ids = [0]
    pending = []

    def take(count):
        ids[0] += count
        return ids[0] - count

    def copy(src, dst, device, recv=None, start=True):
        num = take(1)
        op = pltpu.make_async_remote_copy(
            src_ref=src,
            dst_ref=dst,
            send_sem=send_sem.at[num],
            recv_sem=recv_sem.at[num if recv is None else recv],
            device_id=device,
            device_id_type=MESH,
        )
        if start:
            op.start()
            pending.append(op)
        return op

    def arrival(dst, recv):
        return pltpu.make_async_remote_copy(
            src_ref=dst,
            dst_ref=dst,
            send_sem=send_sem.at[0],
            recv_sem=recv_sem.at[recv],
            device_id=dev(c=oc),
            device_id_type=MESH,
        )

    barrier = pltpu.get_barrier_semaphore()
    friends = [dev(c=oc)]
    friends += [dev(h=ring(h, o)) for o in (1, 2, 3)]
    friends += [dev(y=ring(y, o)) for o in (1, 2, 3)]
    friends += [zdev(ring(zi, o, 8)) for o in range(1, 8)]
    friends += [dev(h=ring(h, o), c=oc) for o in (1, 2, 3)]
    for friend in friends:
        pl.semaphore_signal(barrier, inc=1, device_id=friend, device_id_type=MESH)

    owner = lax.div(q, 4)
    inner = lax.rem(q, 4) * 64 + lax.broadcasted_iota(jnp.int32, (64, 1024), 0)
    block = lax.broadcasted_iota(jnp.int32, (64, 1024), 1) // B
    for lev, (low, pat, wid) in enumerate(((low2, pat2, wid2), (low1, pat1, wid1))):
        present = jnp.zeros((64, 1024), F32)
        for b in range(4):
            there = pat[owner, 4 * r + b].astype(F32)
            present = jnp.where(block == b, there, present)
        keep = jnp.where(inner < wid[owner], present, 0.0)
        lt[lev] = low[...] * keep
    row = lax.broadcasted_iota(jnp.int32, (B, B), 0)
    col = lax.broadcasted_iota(jnp.int32, (B, B), 1)
    inside = jnp.where(row < wid1[r], 1.0, 0.0) * jnp.where(col < wid2[par[r]], 1.0, 0.0)
    lpt[...] = lpar[0].T * inside

    pl.semaphore_wait(barrier, len(friends))

    hl, hr = dev(h=ring(h, -1)), dev(h=ring(h, 1))
    yl, yr = dev(y=ring(y, -1)), dev(y=ring(y, 1))
    sib, pair = dev(c=oc), dev(w=1 - w)
    mine = 2 * y + w
    theirs = 2 * y + 1 - w
    ml, mr, mf = 2 * ring(y, -1), 2 * ring(y, 1), 2 * ring(y, 2)
    top, bot = pl.ds(0, 512), pl.ds(512, 512)

    def split_l(lev, m):
        hi, lo = split(lg[lev, m])
        lh[lev, m] = hi
        ll[lev, m] = lo

    def send_own(lev):
        return (
            copy(lt.at[lev], lg.at[lev, mine], yr),
            copy(lt.at[lev], lg.at[lev, mine], yl),
        )

    def send_pair(lev):
        return (
            copy(lg.at[lev, theirs], lg.at[lev, theirs], yr),
            copy(lg.at[lev, theirs], lg.at[lev, theirs], yl),
        )

    def forward_l(lev, ops, which):
        near, far = pl.ds(0, 32), pl.ds(32, 32)
        ops[0].wait_recv()
        one = copy(lg.at[lev, ml + which, near], lg.at[lev, ml + which, near], yr)
        ops[1].wait_recv()
        two = copy(lg.at[lev, mr + which, far], lg.at[lev, mr + which, far], yl)
        return one, two

    def send_a(half):
        cols = pl.ds(128 * half, 128)
        return (
            copy(a.at[top, cols], ag.at[0, half, top], hr),
            copy(a.at[bot, cols], ag.at[1, half, bot], hl),
            copy(a.at[bot, cols], ag.at[0, half, bot], hr),
            copy(a.at[top, cols], ag.at[1, half, top], hl),
        )

    def forward_a(half, ops):
        ops[0].wait_recv()
        one = copy(ag.at[0, half, top], ag.at[2, half, top], hr)
        ops[1].wait_recv()
        two = copy(ag.at[1, half, bot], ag.at[2, half, bot], hl)
        return one, two

    def split_a(half, rel):
        hi, lo = split(a[:, 128 * half : 128 * half + 128] if rel == 0 else ag[rel - 1, half])
        cols = slice(128 * (rel % 2), 128 * (rel % 2) + 128)
        ah[half, rel // 2, :, cols] = hi
        al[half, rel // 2, :, cols] = lo

    w2 = copy(lt.at[0], lg.at[0, mine], pair)
    o2 = send_own(0)
    a0 = send_a(0)
    d2c = copy(d2, d2s, sib)

    rows32 = pl.ds(pl.multiple_of(mine * 32, 32), 32)
    rows64 = pl.ds(pl.multiple_of(y * 64, 64), 64)
    lp_recv = ids[0]
    lp_ops = [
        copy(lpt.at[rows32], lpn.at[rows32], dev(k=ring(k, o)), recv=lp_recv, start=False)
        for o in (1, 2, 3)
    ]

    @pl.when(h == k)
    def _():
        lpn[rows32] = lpt[rows32]
        for op in lp_ops:
            op.start()

    lg[0, mine] = lt[0]
    lg[1, mine] = lt[1]
    split_l(0, mine)
    split_l(1, mine)
    split_a(0, 0)
    split_a(1, 0)
    w2.wait_recv()
    p2 = send_pair(0)
    f2 = forward_l(0, o2, w)
    split_l(0, theirs)
    split_l(0, ml + w)
    split_l(0, mr + w)
    fa0 = forward_a(0, a0)
    a1 = send_a(1)
    w1 = copy(lt.at[1], lg.at[1, mine], pair)
    e2 = forward_l(0, p2, 1 - w)
    o1 = send_own(1)
    split_l(0, ml + 1 - w)
    split_l(0, mr + 1 - w)
    a0[2].wait_recv()
    split_a(0, 1)
    a0[3].wait_recv()
    split_a(0, 2)
    for op in f2:
        op.wait_recv()
    split_l(0, mf + w)
    for op in e2:
        op.wait_recv()
    split_l(0, mf + 1 - w)

    cy = lax.div(y, 2)
    off = pl.multiple_of(lax.rem(mine, 4) * B, B)
    l_ops = [copy(lsnd.at[lev], lloc.at[lev], sib, start=False) for lev in range(2)]

    def share(lev):
        @pl.when(c == cy)
        def _():
            lsnd[lev] = lg[lev, pl.ds(4 * oc, 4), :, pl.ds(off, B)].reshape(B, B)
            l_ops[lev].start()
            lloc[lev] = lg[lev, pl.ds(4 * c, 4), :, pl.ds(off, B)].reshape(B, B)

        @pl.when(c != cy)
        def _():
            l_ops[lev].wait_recv()

    kp, km, ko = ring(k, 1), ring(k, -1), ring(k, 2)
    zp, zm = dev(k=kp), dev(k=km)
    up, dn = pl.ds(0, 128), pl.ds(128, 128)
    slots = (h, ring(h, -1), ring(h, 1), ring(h, 2))

    def product(lev, half, duo):
        def part(parity):
            left_h = lh[lev, pl.ds(4 * parity, 4)].reshape(B, 1024)
            left_l = ll[lev, pl.ds(4 * parity, 4)].reshape(B, 1024)
            value = dot3(left_h, left_l, ah[half, duo], al[half, duo])
            for side in range(2):
                pp[lev, half, slots[2 * duo + side], parity] = value[:, 128 * side : 128 * side + 128]

        part(oc)
        ops = []
        for side in range(2):
            slot = slots[2 * duo + side]
            ops.append(copy(pp.at[lev, half, slot, oc], rc.at[lev, half, slot], sib))
        part(c)
        return [(lev, half, slots[2 * duo + side], ops[side]) for side in range(2)]

    def add_cores(parts):
        for lev, half, slot, op in parts:
            op.wait_recv()
            pp[lev, half, slot, c] += rc[lev, half, slot]

    def reduce_start(lev, half):
        mine_of = pp.at[lev, half]
        return [
            copy(mine_of.at[ko, c, up], r_in.at[lev, half, 0], zp),
            copy(mine_of.at[ko, c, dn], r_in.at[lev, half, 1], zm),
            copy(mine_of.at[kp, c, dn], pl_in.at[lev, half, 0], zp),
            copy(mine_of.at[km, c, up], pl_in.at[lev, half, 1], zm),
        ]

    def relay(lev, half, ops):
        ops[0].wait_recv()
        s_out[lev, half, 0] = r_in[lev, half, 0] + pp[lev, half, kp, c, up]
        ops.append(copy(s_out.at[lev, half, 0], f_in.at[lev, half, 0], zp))
        ops[1].wait_recv()
        s_out[lev, half, 1] = r_in[lev, half, 1] + pp[lev, half, km, c, dn]
        ops.append(copy(s_out.at[lev, half, 1], f_in.at[lev, half, 1], zm))

    def total(lev, half, ops):
        for op in ops[2:]:
            op.wait_recv()
        upper = pp[lev, half, k, c, up] + f_in[lev, half, 0] + pl_in[lev, half, 1]
        lower = pp[lev, half, k, c, dn] + f_in[lev, half, 1] + pl_in[lev, half, 0]
        return jnp.concatenate([upper, lower], axis=0)

    class Place:
        def __init__(self, piece, buf, out):
            tz, tx = t_z.at[piece], t_x.at[piece]
            self.buf, self.out, self.tz, self.tx = buf, out, tz, tx
            self.z_base, self.x_base = take(4), take(4)
            self.got_z, self.got_x = take(1), take(1)
            self.via_z = copy(
                buf.at[up], tz.at[k], dev(k=h), recv=self.z_base + ring(k, 4 - h), start=False
            )
            self.via_x = copy(
                buf.at[dn], tx.at[h], dev(h=k), recv=self.x_base + ring(h, 4 - k), start=False
            )
            self.on_z, self.on_x = [], []
            for o in (1, 2, 3):
                v = ring(k, o)
                self.on_z.append(
                    copy(tz.at[v], out.at[up], dev(h=v), recv=self.got_z, start=False)
                )
                self.on_x.append(
                    copy(tx.at[v], out.at[dn], dev(k=v), recv=self.got_x, start=False)
                )

        def begin_x(self):
            @pl.when(h != k)
            def _():
                self.via_x.start()

            @pl.when(h == k)
            def _():
                self.out[...] = self.buf[...]

        def begin_z(self):
            @pl.when(h != k)
            def _():
                self.via_z.start()

        def pass_x(self):
            @pl.when(h == k)
            def _():
                for o in (1, 2, 3):
                    arrival(self.tx.at[ring(k, o)], self.x_base + o).wait_recv()
                    self.on_x[o - 1].start()

        def pass_z(self):
            @pl.when(h == k)
            def _():
                for o in (1, 2, 3):
                    arrival(self.tz.at[ring(k, o)], self.z_base + o).wait_recv()
                    self.on_z[o - 1].start()

        def finish(self):
            @pl.when(h != k)
            def _():
                self.via_z.wait_send()
                self.via_x.wait_send()
                arrival(self.out.at[up], self.got_z).wait_recv()
                arrival(self.out.at[dn], self.got_x).wait_recv()

            @pl.when(h == k)
            def _():
                for op in self.on_z + self.on_x:
                    op.wait_send()

    left, right = pl.ds(0, 128), pl.ds(128, 128)
    place_20 = Place(0, x2.at[:, left], u2.at[:, left])
    place_21 = Place(1, x2.at[:, right], u2.at[:, right])
    place_10 = Place(2, x1.at[:, left], u1.at[:, left])
    place_11 = Place(3, x1.at[:, right], u1.at[:, right])

    def x2_half(half, ops):
        value = -total(0, half, ops)
        x2[:, 128 * half : 128 * half + 128] = value
        x2all[half, n] = value

    duo = product(0, 0, 0)
    for op in fa0:
        op.wait_recv()
    split_a(0, 3)
    add_cores(duo + product(0, 0, 1))
    rs00 = reduce_start(0, 0)
    share(0)
    w1.wait_recv()
    p1 = send_pair(1)
    f1 = forward_l(1, o1, w)
    split_l(1, theirs)
    split_l(1, ml + w)
    split_l(1, mr + w)
    fa1 = forward_a(1, a1)
    relay(0, 0, rs00)
    e1 = forward_l(1, p1, 1 - w)

    @pl.when(h != k)
    def _():
        lp_ops[0].wait_recv()

    lp_w = copy(lpn.at[rows32], lpn.at[rows32], pair)
    split_l(1, ml + 1 - w)
    split_l(1, mr + 1 - w)
    a1[2].wait_recv()
    split_a(1, 1)
    a1[3].wait_recv()
    split_a(1, 2)
    duo = product(0, 1, 0)
    for op in f1:
        op.wait_recv()
    split_l(1, mf + w)
    x2_half(0, rs00)
    place_20.begin_x()
    place_20.begin_z()
    for op in fa1:
        op.wait_recv()
    split_a(1, 3)
    add_cores(duo + product(0, 1, 1))
    rs01 = reduce_start(0, 1)
    for op in e1:
        op.wait_recv()
    split_l(1, mf + 1 - w)

    def gather_start(buf):
        return copy(buf.at[n], buf.at[n], hr), copy(buf.at[n], buf.at[n], hl), copy(
            buf.at[n], buf.at[n], sib
        )

    def gather_mid(buf, ops):
        left, right = 2 * ring(h, -1) + c, 2 * ring(h, 1) + c
        ops[0].wait_recv()
        one = copy(buf.at[left, up], buf.at[left, up], hr)
        sib_l = copy(buf.at[left], buf.at[left], sib)
        ops[1].wait_recv()
        two = copy(buf.at[right, dn], buf.at[right, dn], hl)
        sib_r = copy(buf.at[right], buf.at[right], sib)
        return one, two, ops[2], sib_l, sib_r

    def gather_end(buf, ops):
        opp = 2 * ring(h, 2) + c
        ops[0].wait_recv()
        ops[1].wait_recv()
        last = copy(buf.at[opp], buf.at[opp], sib)
        for op in ops[2:]:
            op.wait_recv()
        last.wait_recv()

    x20 = gather_start(x2all.at[0])
    lp_w.wait_recv()
    lp_y = [copy(lpn.at[rows64], lpn.at[rows64], dev(y=ring(y, o))) for o in (1, 2, 3)]
    duo = product(1, 0, 0)
    add_cores(duo + product(1, 0, 1))
    rs10 = reduce_start(1, 0)
    relay(0, 1, rs01)
    duo = product(1, 1, 0)
    add_cores(duo + product(1, 1, 1))
    rs11 = reduce_start(1, 1)
    share(1)
    place_20.pass_x()
    place_20.pass_z()
    x20 = gather_mid(x2all.at[0], x20)
    relay(1, 0, rs10)

    own8 = pl.ds(pl.multiple_of(zi * 8, 8), 8)

    class Chain:
        def __init__(self, red, ry, yr, rz, zr, gz, fin):
            self.bufs = (red, ry, yr, rz, zr, gz, fin)

        def y_start(self):
            red, ry = self.bufs[:2]
            self.ops = []
            for o in (1, 2, 3):
                to = ring(y, o)
                part = pl.ds(pl.multiple_of(to * 64, 64), 64)
                self.ops.append(copy(red.at[:, part], ry.at[o - 1], dev(y=to)))

        def z_start(self):
            red, ry, yr, rz = self.bufs[:4]
            acc = red[:, rows64, :]
            for o in range(3):
                self.ops[o].wait_recv()
                acc = acc + ry[o]
            yr[...] = acc
            self.ops = []
            for o in range(1, 8):
                to = ring(zi, o, 8)
                part = pl.ds(pl.multiple_of(to * 8, 8), 8)
                self.ops.append(copy(yr.at[:, part], rz.at[o - 1], zdev(to)))

        def plane_start(self, less=None):
            yr, rz, zr, gz = self.bufs[2:6]
            acc = yr[:, own8, :]
            for o in range(7):
                self.ops[o].wait_recv()
                acc = acc + rz[o]
            zr[...] = acc if less is None else acc - less[None]
            self.base = take(8)
            self.sends = []
            for v in (0, 1):
                op = copy(
                    zr, gz.at[:, own8], dev(k=h, w=v), recv=self.base + zi, start=False
                )
                self.sends.append(op)

                @pl.when(2 * h + v != zi)
                def _(op=op):
                    op.start()

        def x_send(self):
            zr, gz = self.bufs[4:6]
            got = ids[0]
            self.spread = [
                copy(gz, gz, dev(h=ring(h, o)), recv=got, start=False) for o in (1, 2, 3)
            ]

            @pl.when(h == k)
            def _():
                gz[:, own8, :] = zr[...]
                for o in range(1, 8):
                    frm = ring(zi, o, 8)
                    part = pl.ds(pl.multiple_of(frm * 8, 8), 8)
                    arrival(gz.at[:, part], self.base + frm).wait_recv()
                for op in self.spread:
                    op.start()

        def x_recv(self):
            @pl.when(h != k)
            def _():
                self.spread[0].wait_recv()

        def y_spread(self):
            gz, fin = self.bufs[5:]
            self.ops = [copy(gz, fin.at[:, rows64], dev(y=ring(y, o))) for o in (1, 2, 3)]
            fin[:, rows64, :] = gz[...]

        def finish(self):
            for op in self.ops:
                op.wait_recv()

        def drain(self):
            for v in (0, 1):

                @pl.when(2 * h + v != zi)
                def _(v=v):
                    self.sends[v].wait_send()

            @pl.when(h == k)
            def _():
                for op in self.spread:
                    op.wait_send()

    sum_g = Chain(red_g, ry_g, yr_g, rz_g, zr_g, gz_g, fin_g)
    sum_f = Chain(red_f, ry_f, yr_f, rz_f, zr_f, gz_f, fin_f)
    sum_s = Chain(red_s, ry_s, yr_s, rz_s, zr_s, gz_s, fin_s)
    x2_half(1, rs01)
    place_21.begin_x()
    x21 = gather_start(x2all.at[1])
    red_g[0] = mm(lloc[0], x2[...], NT)
    sum_g.y_start()
    gather_end(x2all.at[0], x20)
    relay(1, 1, rs11)
    for op in lp_y:
        op.wait_recv()
    parent = par[n]
    lp_h, lp_l = split(lpn[...])
    d2c.wait_recv()
    here = jnp.where(parent == r, 1.0, 0.0)
    beside = jnp.where(parent == 2 * k + oc, 1.0, 0.0)
    own_rows = dot3(*split(d2[0, rows32] * here + d2s[0, rows32] * beside), lp_h, lp_l, NT)
    sum_g.z_start()
    x21 = gather_mid(x2all.at[1], x21)
    sum_g.plane_start()
    g_all[n] = zr_g[0]
    slices = [copy(g_all.at[n], g_all.at[n], sib)]
    for o in (1, 2, 3):
        for core in (c, oc):
            slices.append(copy(g_all.at[n], g_all.at[n], dev(h=ring(h, o), c=core)))
    gather_end(x2all.at[1], x21)
    x2p = jnp.concatenate([x2all[0, parent], x2all[1, parent]], axis=1)
    red_f[0] = mm(x2p, lloc[1], NT)
    red_f[0, rows32] += own_rows
    sum_f.y_start()
    correction = dot3(lp_h, lp_l, *split(x2p))
    sum_g.x_send()
    x1[:, 0:128] = -total(1, 0, rs10) - correction[:, 0:128]
    x1[:, 128:256] = -total(1, 1, rs11) - correction[:, 128:256]
    place_10.begin_x()
    place_11.begin_x()
    red_s[0] = mm(lloc[1], x1[...], NT)
    sum_s.y_start()
    sum_f.z_start()
    sum_g.x_recv()
    sum_g.y_spread()
    sum_s.z_start()
    for op in slices:
        op.wait_recv()
    sum_f.plane_start(dot3(*split(g_all[parent]), lp_h, lp_l, NT))
    sum_s.plane_start()
    later = (place_21, place_10, place_11)
    for move in later:
        move.begin_z()
        move.pass_x()
    sum_f.x_send()
    sum_s.x_send()
    sum_f.x_recv()
    sum_f.y_spread()
    sum_g.finish()
    g2o[...] = d2[0] - fin_g[0]
    sum_s.x_recv()
    sum_s.y_spread()
    for move in later:
        move.pass_z()
    sum_f.finish()
    pb = -fin_f[0]
    pbo[...] = pb
    update = d1[0] - mm(lpt[...], pb)
    sum_s.finish()
    g1o[...] = update - fin_s[0]
    place_20.finish()
    for move in later:
        move.finish()

    for chain in (sum_g, sum_f, sum_s):
        chain.drain()

    @pl.when(h == k)
    def _():
        for op in lp_ops:
            op.wait_send()

    @pl.when(c == cy)
    def _():
        for op in l_ops:
            op.wait_send()

    for op in pending:
        op.wait_send()
    assert ids[0] <= SEMS


def settle(*refs):
    for src, dst in zip(refs[:5], refs[5:]):
        dst[...] = src[...].reshape(dst.shape)


def per_device(
    inverse_anc,
    lower_two,
    pattern_two,
    widths_two,
    dinv_two,
    lower_one,
    pattern_one,
    widths_one,
    parent_one,
    lower_par,
    dinv_one,
):
    vmem = pl.BlockSpec(memory_space=pltpu.VMEM)
    smem = pl.BlockSpec(memory_space=pltpu.SMEM)
    square = jax.ShapeDtypeStruct((B, B), F32)
    cube = jax.ShapeDtypeStruct((1, B, B), F32)

    def chain(count):
        return [
            pltpu.VMEM((count, B, B), F32),
            pltpu.VMEM((3, count, 64, B), F32),
            pltpu.VMEM((count, 64, B), F32),
            pltpu.VMEM((7, count, 8, B), F32),
            pltpu.VMEM((count, 8, B), F32),
            pltpu.VMEM((count, 64, B), F32),
            pltpu.VMEM((count, B, B), F32),
        ]

    outs = pl.pallas_call(
        kernel,
        out_shape=[square] * 5,
        in_specs=[smem] * 5 + [vmem] * 6,
        out_specs=[vmem] * 5,
        scratch_shapes=[
            pltpu.VMEM((3, 2, 1024, 128), F32),
            pltpu.VMEM((2, 64, 1024), F32),
            pltpu.VMEM((2, 8, 64, 1024), F32),
            pltpu.VMEM((2, 8, 64, 1024), BF16),
            pltpu.VMEM((2, 8, 64, 1024), BF16),
            pltpu.VMEM((2, 2, 1024, B), BF16),
            pltpu.VMEM((2, 2, 1024, B), BF16),
            pltpu.VMEM((2, 2, 4, 2, B, 128), F32),
            pltpu.VMEM((2, 2, 4, B, 128), F32),
            pltpu.VMEM((2, 2, 2, 128, 128), F32),
            pltpu.VMEM((2, 2, 2, 128, 128), F32),
            pltpu.VMEM((2, 2, 2, 128, 128), F32),
            pltpu.VMEM((2, 2, 2, 128, 128), F32),
            pltpu.VMEM((2, B, B), F32),
            pltpu.VMEM((2, B, B), F32),
            pltpu.VMEM((B, B), F32),
            pltpu.VMEM((B, B), F32),
            pltpu.VMEM((1, B, B), F32),
            pltpu.VMEM((2, 8, B, 128), F32),
            pltpu.VMEM((B, B), F32),
            pltpu.VMEM((B, B), F32),
            pltpu.VMEM((4, 4, 128, 128), F32),
            pltpu.VMEM((4, 4, 128, 128), F32),
            pltpu.VMEM((8, 8, B), F32),
            *chain(1),
            *chain(1),
            *chain(1),
            pltpu.SemaphoreType.DMA((SEMS,)),
            pltpu.SemaphoreType.DMA((SEMS,)),
        ],
        compiler_params=pltpu.CompilerParams(
            collective_id=0, has_side_effects=True, vmem_limit_bytes=56 * 1024 * 1024
        ),
    )(
        parent_one,
        widths_two,
        widths_one,
        pattern_two.T,
        pattern_one.T,
        inverse_anc,
        lower_two.T,
        lower_one.T,
        lower_par,
        dinv_two,
        dinv_one,
    )
    u2, g2, u1, pb, g1 = pl.pallas_call(
        settle,
        out_shape=[square, cube, square, cube, cube],
        in_specs=[vmem] * 5,
        out_specs=[vmem] * 5,
    )(outs[0], outs[2], outs[1], outs[3], outs[4])
    return u2, g2, u1, pb, g1


def solution(mesh):
    in_specs = (
        P("prow", "pcol"),
        P("prow", "pcol"),
        P(),
        P(),
        P("prow", None, None),
        P("prow", "pcol"),
        P(),
        P(),
        P(),
        P("prow", None, None),
        P("prow", None, None),
    )
    out_specs = (
        P("prow", "pcol"),
        P("prow", None, None),
        P("prow", "pcol"),
        P("prow", None, None),
        P("prow", None, None),
    )
    return jax.shard_map(
        per_device, mesh=mesh, in_specs=in_specs, out_specs=out_specs, check_vma=False
    )
```

time: 151 us -> 135 us (0.89)
  Pallas kernels: 143 us -> 134 us
  local copies, waits for them, and re-layouts: 5.05 us -> 0 us
    pallas_call x1, Pallas kernels: 141 us -> 131 us  [per_device(): pl.pallas_call(kernel, out_shape=[square] * 5, in_specs=[smem] * 5 + [vme...]
    unnamed x8 -> x0, local copies, waits for them, and re-layouts: 5.05 us -> none
where the time goes in v3:
time: 135 us; the launch traced here: 134 us
  Pallas kernels  134 us (99%)
    pallas_call x1, Pallas kernels, per_device(): pl.pallas_call(kernel, out_shape=[square] * 5, in_specs=[smem] * 5 + [vme...  131 us

profile of v3, /device:TPU:4, one launch (start us, length us, event | category | flops | bytes accessed | tf_op | source)
XLA Modules:
  0.0 134.4 jit_solution(4499456875548888256)
XLA Ops:
  0.6 131.4 %shard_map.146 = (f32[256,256]{1,0:T(8,128)}, f32[256,256]{1,0:T(8,128)}, f32[256,256]{1,0:T(8,128)}, f32[256,256]{1,0:T(8,128)}, f32[256,256]{1,0:T(8,128)}) custom-call(s32[8]{0:T(128)} %par.1, s32[8]{0:T(128)} %wid2.1, s32[8]{0:T(128)} %wid1.1, s32[8,32]{1,0:T(8,128)} %bitcast.6, s32[8,32]{1,0:T(8,128)} %bitcast.7, f32[1024,256]{1,0:T(8,128)} %a.1, ...), custom_call_target="tpu_custom_call" | custom-call | tf_op jit(solution)/shard_map/pallas_call | solution.py:656
  132.1 2.3 %shard_map.147 = (f32[256,256]{1,0:T(8,128)}, f32[1,256,256]{2,1,0:T(8,128)}, f32[256,256]{1,0:T(8,128)}, f32[1,256,256]{2,1,0:T(8,128)}, f32[1,256,256]{2,1,0:T(8,128)}) custom-call(f32[256,256]{1,0:T(8,128)} %get-tuple-element.10.refs_0_, f32[256,256]{1,0:T(8,128)} %get-tuple-element.11.refs_1_, f32[256,256]{1,0:T(8,128)} %get-tuple-element.12.refs_2_, ...), custom_call_target="tpu_custom_call" | custom-call | tf_op jit(solution)/shard_map/pallas_call | solution.py:708

commit v4 on v3

--- a/solution.py
+++ b/solution.py
@@ -535,11 +535,14 @@
     sum_s = Chain(red_s, ry_s, yr_s, rz_s, zr_s, gz_s, fin_s)
     x2_half(1, rs01)
     place_21.begin_x()
+    place_21.begin_z()
     x21 = gather_start(x2all.at[1])
     red_g[0] = mm(lloc[0], x2[...], NT)
     sum_g.y_start()
     gather_end(x2all.at[0], x20)
+    x21 = gather_mid(x2all.at[1], x21)
     relay(1, 1, rs11)
+    sum_g.z_start()
     for op in lp_y:
         op.wait_recv()
     parent = par[n]
@@ -548,20 +551,19 @@
     here = jnp.where(parent == r, 1.0, 0.0)
     beside = jnp.where(parent == 2 * k + oc, 1.0, 0.0)
     own_rows = dot3(*split(d2[0, rows32] * here + d2s[0, rows32] * beside), lp_h, lp_l, NT)
-    sum_g.z_start()
-    x21 = gather_mid(x2all.at[1], x21)
+    gather_end(x2all.at[1], x21)
+    x2p = jnp.concatenate([x2all[0, parent], x2all[1, parent]], axis=1)
+    red_f[0] = mm(x2p, lloc[1], NT)
+    red_f[0, rows32] += own_rows
+    sum_f.y_start()
+    correction = dot3(lp_h, lp_l, *split(x2p))
     sum_g.plane_start()
     g_all[n] = zr_g[0]
     slices = [copy(g_all.at[n], g_all.at[n], sib)]
     for o in (1, 2, 3):
         for core in (c, oc):
             slices.append(copy(g_all.at[n], g_all.at[n], dev(h=ring(h, o), c=core)))
-    gather_end(x2all.at[1], x21)
-    x2p = jnp.concatenate([x2all[0, parent], x2all[1, parent]], axis=1)
-    red_f[0] = mm(x2p, lloc[1], NT)
-    red_f[0, rows32] += own_rows
-    sum_f.y_start()
-    correction = dot3(lp_h, lp_l, *split(x2p))
+    sum_f.z_start()
     sum_g.x_send()
     x1[:, 0:128] = -total(1, 0, rs10) - correction[:, 0:128]
     x1[:, 128:256] = -total(1, 1, rs11) - correction[:, 128:256]
@@ -569,7 +571,8 @@
     place_11.begin_x()
     red_s[0] = mm(lloc[1], x1[...], NT)
     sum_s.y_start()
-    sum_f.z_start()
+    place_21.pass_x()
+    place_21.pass_z()
     sum_g.x_recv()
     sum_g.y_spread()
     sum_s.z_start()
@@ -577,10 +580,10 @@
         op.wait_recv()
     sum_f.plane_start(dot3(*split(g_all[parent]), lp_h, lp_l, NT))
     sum_s.plane_start()
-    later = (place_21, place_10, place_11)
-    for move in later:
-        move.begin_z()
-        move.pass_x()
+    place_10.begin_z()
+    place_11.begin_z()
+    place_10.pass_x()
+    place_11.pass_x()
     sum_f.x_send()
     sum_s.x_send()
     sum_f.x_recv()
@@ -589,8 +592,8 @@
     g2o[...] = d2[0] - fin_g[0]
     sum_s.x_recv()
     sum_s.y_spread()
-    for move in later:
-        move.pass_z()
+    place_10.pass_z()
+    place_11.pass_z()
     sum_f.finish()
     pb = -fin_f[0]
     pbo[...] = pb
@@ -598,7 +601,7 @@
     sum_s.finish()
     g1o[...] = update - fin_s[0]
     place_20.finish()
-    for move in later:
+    for move in (place_21, place_10, place_11):
         move.finish()
 
     for chain in (sum_g, sum_f, sum_s):

time: 135 us -> 128 us (0.948)
  Pallas kernels: 134 us -> 127 us
    pallas_call x1, Pallas kernels: 131 us -> 125 us  [per_device(): pl.pallas_call(kernel, out_shape=[square] * 5, in_specs=[smem] * 5 + [vme...]
where the time goes in v4:
time: 128 us
  Pallas kernels  127 us (99%)
    pallas_call x1, Pallas kernels, per_device(): pl.pallas_call(kernel, out_shape=[square] * 5, in_specs=[smem] * 5 + [vme...  125 us

profile of v4, /device:TPU:4, one launch (start us, length us, event | category | flops | bytes accessed | tf_op | source)
XLA Modules:
  0.0 127.8 jit_solution(8837398261205202899)
XLA Ops:
  0.6 124.8 %shard_map.146 = (f32[256,256]{1,0:T(8,128)}, f32[256,256]{1,0:T(8,128)}, f32[256,256]{1,0:T(8,128)}, f32[256,256]{1,0:T(8,128)}, f32[256,256]{1,0:T(8,128)}) custom-call(s32[8]{0:T(128)} %par.1, s32[8]{0:T(128)} %wid2.1, s32[8]{0:T(128)} %wid1.1, s32[8,32]{1,0:T(8,128)} %bitcast.6, s32[8,32]{1,0:T(8,128)} %bitcast.7, f32[1024,256]{1,0:T(8,128)} %a.1, ...), custom_call_target="tpu_custom_call" | custom-call | tf_op jit(solution)/shard_map/pallas_call | solution.py:659
  125.5 2.3 %shard_map.147 = (f32[256,256]{1,0:T(8,128)}, f32[1,256,256]{2,1,0:T(8,128)}, f32[256,256]{1,0:T(8,128)}, f32[1,256,256]{2,1,0:T(8,128)}, f32[1,256,256]{2,1,0:T(8,128)}) custom-call(f32[256,256]{1,0:T(8,128)} %get-tuple-element.10.refs_0_, f32[256,256]{1,0:T(8,128)} %get-tuple-element.11.refs_1_, f32[256,256]{1,0:T(8,128)} %get-tuple-element.12.refs_2_, ...), custom_call_target="tpu_custom_call" | custom-call | tf_op jit(solution)/shard_map/pallas_call | solution.py:711

commit v5 on v4

--- a/solution.py
+++ b/solution.py
@@ -31,14 +31,14 @@
 
 
 def kernel(
-    par, wid2, wid1, pat2, pat1, a, low2, low1, lpar, d2, d1,
+    par, wid2, wid1, pat2, pat1, a_hbm, low2, low1, lpar, d2, d1,
     u2, u1, g2o, pbo, g1o,
-    ag, lt, lg, lh, ll, ah, al, pp, rc, r_in, pl_in, f_in, s_out,
+    a, ag, lt, lg, lh, ll, ah, al, pp, rc, r_in, pl_in, f_in, s_out,
     lloc, lsnd, lpt, lpn, d2s, x2all, x2, x1, t_z, t_x, g_all,
     red_g, ry_g, yr_g, rz_g, zr_g, gz_g, fin_g,
     red_f, ry_f, yr_f, rz_f, zr_f, gz_f, fin_f,
     red_s, ry_s, yr_s, rz_s, zr_s, gz_s, fin_s,
-    send_sem, recv_sem,
+    send_sem, recv_sem, load_sem,
 ):
     r, q = lax.axis_index("prow"), lax.axis_index("pcol")
     k, c = lax.div(r, 2), lax.rem(r, 2)
@@ -97,6 +97,8 @@
     for friend in friends:
         pl.semaphore_signal(barrier, inc=1, device_id=friend, device_id_type=MESH)
 
+    load = pltpu.make_async_copy(a_hbm, a, load_sem)
+    load.start()
     owner = lax.div(q, 4)
     inner = lax.rem(q, 4) * 64 + lax.broadcasted_iota(jnp.int32, (64, 1024), 0)
     block = lax.broadcasted_iota(jnp.int32, (64, 1024), 1) // B
@@ -112,6 +114,7 @@
     inside = jnp.where(row < wid1[r], 1.0, 0.0) * jnp.where(col < wid2[par[r]], 1.0, 0.0)
     lpt[...] = lpar[0].T * inside
 
+    load.wait()
     pl.semaphore_wait(barrier, len(friends))
 
     hl, hr = dev(h=ring(h, -1)), dev(h=ring(h, 1))
@@ -322,14 +325,14 @@
         def pass_x(self):
             @pl.when(h == k)
             def _():
-                for o in (1, 2, 3):
+                for o in (2, 1, 3):
                     arrival(self.tx.at[ring(k, o)], self.x_base + o).wait_recv()
                     self.on_x[o - 1].start()
 
         def pass_z(self):
             @pl.when(h == k)
             def _():
-                for o in (1, 2, 3):
+                for o in (2, 1, 3):
                     arrival(self.tz.at[ring(k, o)], self.z_base + o).wait_recv()
                     self.on_z[o - 1].start()
 
@@ -363,6 +366,7 @@
     split_a(0, 3)
     add_cores(duo + product(0, 0, 1))
     rs00 = reduce_start(0, 0)
+    fa1 = forward_a(1, a1)
     share(0)
     w1.wait_recv()
     p1 = send_pair(1)
@@ -370,7 +374,6 @@
     split_l(1, theirs)
     split_l(1, ml + w)
     split_l(1, mr + w)
-    fa1 = forward_a(1, a1)
     relay(0, 0, rs00)
     e1 = forward_l(1, p1, 1 - w)
 
@@ -566,25 +569,25 @@
     sum_f.z_start()
     sum_g.x_send()
     x1[:, 0:128] = -total(1, 0, rs10) - correction[:, 0:128]
+    place_10.begin_x()
+    place_10.begin_z()
     x1[:, 128:256] = -total(1, 1, rs11) - correction[:, 128:256]
-    place_10.begin_x()
     place_11.begin_x()
     red_s[0] = mm(lloc[1], x1[...], NT)
     sum_s.y_start()
     place_21.pass_x()
     place_21.pass_z()
+    for op in slices:
+        op.wait_recv()
+    sum_f.plane_start(dot3(*split(g_all[parent]), lp_h, lp_l, NT))
     sum_g.x_recv()
     sum_g.y_spread()
     sum_s.z_start()
-    for op in slices:
-        op.wait_recv()
-    sum_f.plane_start(dot3(*split(g_all[parent]), lp_h, lp_l, NT))
+    sum_f.x_send()
     sum_s.plane_start()
-    place_10.begin_z()
+    place_10.pass_x()
     place_11.begin_z()
-    place_10.pass_x()
     place_11.pass_x()
-    sum_f.x_send()
     sum_s.x_send()
     sum_f.x_recv()
     sum_f.y_spread()
@@ -623,8 +626,19 @@
 
 
 def settle(*refs):
-    for src, dst in zip(refs[:5], refs[5:]):
-        dst[...] = src[...].reshape(dst.shape)
+    held, in_sem, out_sem = refs[10:]
+    loads, stores = [], []
+    for num in range(5):
+        loads.append(pltpu.make_async_copy(refs[num], held.at[num], in_sem.at[num]))
+        loads[-1].start()
+    for num in range(5):
+        dst = refs[5 + num]
+        to = dst.at[0] if len(dst.shape) == 3 else dst
+        stores.append(pltpu.make_async_copy(held.at[num], to, out_sem.at[num]))
+        loads[num].wait()
+        stores[-1].start()
+    for op in stores:
+        op.wait()
 
 
 def per_device(
@@ -659,9 +673,10 @@
     outs = pl.pallas_call(
         kernel,
         out_shape=[square] * 5,
-        in_specs=[smem] * 5 + [vmem] * 6,
+        in_specs=[smem] * 5 + [pl.BlockSpec(memory_space=pl.ANY)] + [vmem] * 5,
         out_specs=[vmem] * 5,
         scratch_shapes=[
+            pltpu.VMEM((1024, B), F32),
             pltpu.VMEM((3, 2, 1024, 128), F32),
             pltpu.VMEM((2, 64, 1024), F32),
             pltpu.VMEM((2, 8, 64, 1024), F32),
@@ -691,6 +706,7 @@
             *chain(1),
             pltpu.SemaphoreType.DMA((SEMS,)),
             pltpu.SemaphoreType.DMA((SEMS,)),
+            pltpu.SemaphoreType.DMA,
         ],
         compiler_params=pltpu.CompilerParams(
             collective_id=0, has_side_effects=True, vmem_limit_bytes=56 * 1024 * 1024
@@ -711,8 +727,13 @@
     u2, g2, u1, pb, g1 = pl.pallas_call(
         settle,
         out_shape=[square, cube, square, cube, cube],
-        in_specs=[vmem] * 5,
-        out_specs=[vmem] * 5,
+        in_specs=[pl.BlockSpec(memory_space=pl.ANY)] * 5,
+        out_specs=[pl.BlockSpec(memory_space=pl.ANY)] * 5,
+        scratch_shapes=[
+            pltpu.VMEM((5, B, B), F32),
+            pltpu.SemaphoreType.DMA((5,)),
+            pltpu.SemaphoreType.DMA((5,)),
+        ],
     )(outs[0], outs[2], outs[1], outs[3], outs[4])
     return u2, g2, u1, pb, g1
 

time: 128 us -> 127 us (level)
  no operation moved by 1% of the time
where the time goes in v5:
time: 127 us
  Pallas kernels  126 us (99%)
    pallas_call x1, Pallas kernels, per_device(): pl.pallas_call(kernel, out_shape=[square] * 5, in_specs=[smem] * 5 + [pl....  124 us

profile of v5, /device:TPU:4, one launch (start us, length us, event | category | flops | bytes accessed | tf_op | source)
XLA Modules:
  0.0 127.0 jit_solution(4542740372641068010)
XLA Ops:
  0.6 124.2 %shard_map.146 = (f32[256,256]{1,0:T(8,128)}, f32[256,256]{1,0:T(8,128)}, f32[256,256]{1,0:T(8,128)}, f32[256,256]{1,0:T(8,128)}, f32[256,256]{1,0:T(8,128)}) custom-call(s32[8]{0:T(128)} %par.1, s32[8]{0:T(128)} %wid2.1, s32[8]{0:T(128)} %wid1.1, s32[8,32]{1,0:T(8,128)} %bitcast.6, s32[8,32]{1,0:T(8,128)} %bitcast.7, f32[1024,256]{1,0:T(8,128)} %a_hbm.1, ...), custom_call_target="tpu_custom_call" | custom-call | tf_op jit(solution)/shard_map/pallas_call | solution.py:673
  124.9 2.1 %shard_map.147 = (f32[256,256]{1,0:T(8,128)}, f32[1,256,256]{2,1,0:T(8,128)}, f32[256,256]{1,0:T(8,128)}, f32[1,256,256]{2,1,0:T(8,128)}, f32[1,256,256]{2,1,0:T(8,128)}) custom-call(f32[256,256]{1,0:T(8,128)} %get-tuple-element.10.refs_0_, f32[256,256]{1,0:T(8,128)} %get-tuple-element.11.refs_1_, f32[256,256]{1,0:T(8,128)} %get-tuple-element.12.refs_2_, ...), custom_call_target="tpu_custom_call" | custom-call | tf_op jit(solution)/shard_map/pallas_call | solution.py:727

commit v6 on v5

--- a/solution.py
+++ b/solution.py
@@ -571,10 +571,11 @@
     x1[:, 0:128] = -total(1, 0, rs10) - correction[:, 0:128]
     place_10.begin_x()
     place_10.begin_z()
+    near_s = mm(lloc[1, :, 0:128], x1[:, 0:128], NT)
     x1[:, 128:256] = -total(1, 1, rs11) - correction[:, 128:256]
+    red_s[0] = near_s + mm(lloc[1, :, 128:256], x1[:, 128:256], NT)
+    sum_s.y_start()
     place_11.begin_x()
-    red_s[0] = mm(lloc[1], x1[...], NT)
-    sum_s.y_start()
     place_21.pass_x()
     place_21.pass_z()
     for op in slices:

time: 127 us -> 128 us (level)
  no operation moved by 1% of the time
where the time goes in v6:
time: 128 us; the launch traced here: 127 us
  Pallas kernels  127 us (99%)
    pallas_call x1, Pallas kernels, per_device(): pl.pallas_call(kernel, out_shape=[square] * 5, in_specs=[smem] * 5 + [pl....  125 us

profile of v6, /device:TPU:4, one launch (start us, length us, event | category | flops | bytes accessed | tf_op | source)
XLA Modules:
  0.0 127.5 jit_solution(16416594214090607746)
XLA Ops:
  0.6 124.7 %shard_map.146 = (f32[256,256]{1,0:T(8,128)}, f32[256,256]{1,0:T(8,128)}, f32[256,256]{1,0:T(8,128)}, f32[256,256]{1,0:T(8,128)}, f32[256,256]{1,0:T(8,128)}) custom-call(s32[8]{0:T(128)} %par.1, s32[8]{0:T(128)} %wid2.1, s32[8]{0:T(128)} %wid1.1, s32[8,32]{1,0:T(8,128)} %bitcast.6, s32[8,32]{1,0:T(8,128)} %bitcast.7, f32[1024,256]{1,0:T(8,128)} %a_hbm.1, ...), custom_call_target="tpu_custom_call" | custom-call | tf_op jit(solution)/shard_map/pallas_call | solution.py:674
  125.4 2.1 %shard_map.147 = (f32[256,256]{1,0:T(8,128)}, f32[1,256,256]{2,1,0:T(8,128)}, f32[256,256]{1,0:T(8,128)}, f32[1,256,256]{2,1,0:T(8,128)}, f32[1,256,256]{2,1,0:T(8,128)}) custom-call(f32[256,256]{1,0:T(8,128)} %get-tuple-element.10.refs_0_, f32[256,256]{1,0:T(8,128)} %get-tuple-element.11.refs_1_, f32[256,256]{1,0:T(8,128)} %get-tuple-element.12.refs_2_, ...), custom_call_target="tpu_custom_call" | custom-call | tf_op jit(solution)/shard_map/pallas_call | solution.py:728
